TPU v7x, 32 devices: a whole 2x2x4 slice. The times are simulated.
32 devices in a mesh: node: 16 (over z, x, core), feat: 2 (over y).
Axes of the slice: x: 2, y: 2, z: 4, core: 2. Of those that a mesh axis runs over, the one named last changes fastest.
Arguments:
- features: bfloat16 [98304, 256], P('node', 'feat'), may hold values from -6 to 6
- block_cols: int32 [768, 8], P('node', 'feat'), may hold values from 0 to 767, as said below
- tile_vals: bfloat16 [768, 8, 128, 128], P('node', 'feat'), may hold values from -0.1875 to 0.1875
- weight: bfloat16 [256, 256], replicated, may hold values from -0.375 to 0.375
- cotangent: bfloat16 [98304, 256], P('node', 'feat'), may hold values from -6 to 6
Outputs:
- activated: bfloat16 [98304, 256], P('node', 'feat')
- grad_weight: float32 [256, 256], P(None, 'feat')
- grad_feats: bfloat16 [98304, 256], P('node', 'feat')
Inputs may be any that keep to these rules, and one draw needn't show every extreme that they name: `block_cols`: for each index i of node and each slot k, the block rows i * 48 to (i + 1) * 48 - 1 name in slot k at most 3 blocks of the range o * 48 to (o + 1) * 48 - 1 of any one index o, and exactly 3 of some index's range. Tiles may name the same block; their terms add.
All inputs are finite; a program needn't handle non-finite values.
Results may differ from a plain program's by a relative error of at most 0.0071.
Values may be sent and summed in bfloat16 or wider, within the bound.
A program may use at most 128 MiB of HBM per device.

v0:
```python
import math

import jax
import jax.numpy as jnp
from jax import lax
from jax.sharding import PartitionSpec as P


def place_requests(cols_flat, rows_blocks, nodes_dev, cap_all):
    owner_dev = cols_flat // rows_blocks
    local_block = cols_flat % rows_blocks
    matches = (owner_dev[:, None] == jnp.arange(nodes_dev, dtype=jnp.int32)[None, :]).astype(
        jnp.int32
    )
    slot_rank = jnp.sum((jnp.cumsum(matches, axis=0) - matches) * matches, axis=1)
    slot_dest = owner_dev * cap_all + slot_rank
    request = jnp.zeros((nodes_dev * cap_all,), jnp.int32).at[slot_dest].set(local_block)
    return (slot_dest, request.reshape(nodes_dev, cap_all))


def sum_owned(wanted, incoming, rows_blocks):
    flat_ids = wanted.reshape(-1)
    selector = (flat_ids[None, :] == jnp.arange(rows_blocks, dtype=jnp.int32)[:, None]).astype(
        jnp.bfloat16
    )
    flat_in = incoming.reshape(flat_ids.shape[0], -1)
    return jnp.dot(selector, flat_in, preferred_element_type=jnp.float32)


def per_device(features, block_cols, tile_vals, weight, cotangent):
    nodes_dev = lax.axis_size("node")
    rows_blocks = block_cols.shape[0]
    slot_count = block_cols.shape[1]
    tile_size = tile_vals.shape[2]
    feat_width = weight.shape[0]
    col_share = features.shape[1]
    capacity = max(2, (rows_blocks + nodes_dev - 1) // nodes_dev)
    col_index = lax.axis_index("feat")
    weight_cols = lax.dynamic_slice_in_dim(weight, col_index * col_share, col_share, 1)
    whole_rows = lax.all_gather(features, "feat", axis=1, tiled=True)
    cap_all = slot_count * capacity
    slot_dest, request = place_requests(block_cols.reshape(-1), rows_blocks, nodes_dev, cap_all)
    wanted = lax.all_to_all(request, "node", split_axis=0, concat_axis=0, tiled=True)
    served = whole_rows.reshape(rows_blocks, tile_size, feat_width)[wanted]
    fetched = lax.all_to_all(served, "node", split_axis=0, concat_axis=0, tiled=True)
    gathered = fetched.reshape(nodes_dev * cap_all, tile_size, feat_width)[slot_dest]
    gathered = gathered.reshape(rows_blocks, slot_count, tile_size, feat_width)
    partial_value = jnp.einsum(
        "rsab,rsbf->raf", tile_vals, gathered, preferred_element_type=jnp.float32
    )
    partial_value = partial_value.astype(jnp.bfloat16).reshape(rows_blocks * tile_size, feat_width)
    aggregate = lax.psum(partial_value, "feat").astype(jnp.float32).astype(jnp.bfloat16)
    pre_act = jnp.dot(aggregate, weight_cols, preferred_element_type=jnp.float32)
    gate_sig = jax.nn.sigmoid(pre_act)
    activated = (pre_act * gate_sig).astype(jnp.bfloat16)
    grad_pre = (
        cotangent.astype(jnp.float32) * gate_sig * (1.0 + pre_act * (1.0 - gate_sig))
    ).astype(jnp.bfloat16)
    local_weight = jnp.dot(aggregate.T, grad_pre, preferred_element_type=jnp.float32)
    nodes_all = rows_blocks * tile_size * nodes_dev
    grad_weight = lax.psum(local_weight, "node") / math.sqrt(nodes_all)
    grad_wide = lax.all_gather(grad_pre, "feat", axis=1, tiled=True)
    grad_agg = jnp.dot(grad_wide, weight.T, preferred_element_type=jnp.float32).astype(jnp.bfloat16)
    grad_agg = grad_agg.reshape(rows_blocks, tile_size, feat_width)
    contribution = jnp.einsum(
        "rsab,raf->rsbf", tile_vals, grad_agg, preferred_element_type=jnp.float32
    ).astype(jnp.bfloat16)
    outgoing = jnp.zeros((nodes_dev * cap_all, tile_size, feat_width), jnp.bfloat16)
    outgoing = outgoing.at[slot_dest].set(contribution.reshape(-1, tile_size, feat_width))
    outgoing = outgoing.reshape(nodes_dev, cap_all, tile_size, feat_width)
    incoming = lax.all_to_all(outgoing, "node", split_axis=0, concat_axis=0, tiled=True)
    owned_sum = sum_owned(wanted, incoming, rows_blocks).reshape(
        rows_blocks * tile_size, feat_width
    )
    grad_feats = lax.psum_scatter(owned_sum, "feat", scatter_dimension=1, tiled=True).astype(
        jnp.bfloat16
    )
    return (activated, grad_weight, grad_feats)


def solution(mesh):
    return jax.shard_map(
        per_device,
        mesh=mesh,
        in_specs=(
            P("node", "feat"),
            P("node", "feat"),
            P("node", "feat", None, None),
            P(),
            P("node", "feat"),
        ),
        out_specs=(P("node", "feat"), P(None, "feat"), P("node", "feat")),
        check_vma=False,
    )
```

profile of v0, /device:TPU:0, one launch (start us, length us, event | category | flops | bytes accessed | tf_op | source)
XLA Modules:
  0.0 964.9 jit_solution(6483752658343219821)
XLA Ops:
  7.2 0.7 all-gather.3.cloned.1.call-update
  7.9 0.7 broadcast_remainder_fusion
  8.9 0.7 compare_and_fusion
  10.3 0.6 reduce-window.6
  11.3 1.2 scatter_custom_fusion
  12.5 13.6 %all_to_all.22 = s32[16,1,12]{2,1,0:T(1,128)S(1)} all-to-all(s32[16,1,12]{2,1,0:T(1,128)S(1)} %bitcast.61), channel_id=1, replica_groups=mesh['node'=16,'feat'=2] {'node'}, dimensions={0} | all-to-all | bytes 1536 | tf_op jit(solution)/shard_map/all_to_all | solution.py:43
  26.2 31.0 %all-gather.3.cloned.1.call-done = bf16[6144,256]{1,0:T(8,128)(2,1)} async-done(((bf16[6144,128]{1,0:T(8,128)(2,1)}), bf16[6144,256]{1,0:T(8,128)(2,1)}) %all-gather.3.cloned.1.call-update) | async-done | bytes 3145744 | tf_op jit(solution)/shard_map/all_gather | solution.py:40
  57.2 10.1 %gather_fusion = bf16[192,128,256]{2,1,0:T(8,128)(2,1)} fusion(bf16[48,128,256]{2,1,0:T(8,128)(2,1)} %bitcast.56, s32[1024]{0:T(1024)S(1)} %pad_clamp_fusion.1), kind=kCustom, calls=%fused_computation | custom fusion | bytes 25166592 | tf_op jit(solution)/shard_map/gather | solution.py:44
  67.2 5.6 all-to-all-start.1
  73.0 223.7 %all-to-all-done.1 = bf16[16,12,128,256]{3,2,1,0:T(8,128)(2,1)} async-done(((bf16[16,12,128,256]{3,2,1,0:T(8,128)(2,1)}), bf16[16,12,128,256]{3,2,1,0:T(8,128)(2,1)}, u32[]{:S(2)}, u32[]{:S(2)}) %all-to-all-start.1) | async-done | bytes 12582944 | tf_op jit(solution)/shard_map/all_to_all | solution.py:45
  296.6 12.8 %gather_fusion.1 = bf16[192,128,256]{2,1,0:T(8,128)(2,1)} fusion(bf16[192,128,256]{2,1,0:T(8,128)(2,1)} %bitcast.7, s32[1024]{0:T(1024)S(1)} %pad_clamp_fusion), kind=kCustom, calls=%fused_computation.1 | custom fusion | bytes 25166592 | tf_op jit(solution)/shard_map/gather | solution.py:46
  309.4 10.3 %bitcast_convert_fusion = bf16[48,256,128]{1,2,0:T(8,128)(2,1)} fusion(bf16[48,4,128,128]{3,2,1,0:T(8,128)(2,1)} %param.7, bf16[48,4,128,256]{3,2,1,0:T(8,128)(2,1)} %bitcast.53), kind=kOutput, calls=%fused_computation.6 | convolution fusion | flops 1612185600 | bytes 22020096 | tf_op jit(solution)/shard_map/rsab,rsbf->raf/dot_general | solution.py:48
  320.0 133.4 %all-reduce.4.cloned.1.call-done = bf16[6144,256]{1,0:T(8,128)(2,1)} async-done(((bf16[6144,256]{1,0:T(8,128)(2,1)}), bf16[6144,256]{1,0:T(8,128)(2,1)}) %all-reduce.4.cloned.1.call-update) | async-done | bytes 3145744 | tf_op jit(solution)/shard_map/psum | solution.py:52
  453.4 5.3 multiply_convert_fusion
  458.7 45.1 %all-gather.5.cloned.1.call-done = bf16[6144,256]{1,0:T(8,128)(2,1)} async-done(((bf16[6144,128]{1,0:T(8,128)(2,1)}), bf16[6144,256]{1,0:T(8,128)(2,1)}) %all-gather.5.cloned.1.call-update) | async-done | bytes 3145744 | tf_op jit(solution)/shard_map/all_gather | solution.py:62
  503.8 2.9 convolution_convert_fusion
  506.7 9.2 convolution_convert_fusion.1
  515.8 16.6 %copy.27 = bf16[192,128,256]{2,1,0:T(8,128)(2,1)} copy(bf16[192,128,256]{1,2,0:T(8,128)(2,1)} %bitcast.57) | data formatting | bytes 25165824 | tf_op jit(solution)/shard_map/reshape | solution.py:69
  532.4 6.1 broadcast_in_dim.2
  538.5 35.2 %scatter_fusion = bf16[192,128,256]{2,1,0:T(8,128)(2,1)} fusion(bf16[192,128,256]{2,1,0:T(8,128)(2,1)} %broadcast_in_dim.2, s32[192]{0:T(256)S(1)} %bitcast.64, bf16[192,128,256]{2,1,0:T(8,128)(2,1)} %copy.27), kind=kCustom, calls=%fused_computation.3 | custom fusion | bytes 37749504 | tf_op jit(solution)/shard_map/scatter | solution.py:69
  573.7 5.6 all-to-all-start.2
  579.4 0.5 broadcast.159
  579.9 0.7 reduce.5
  580.6 3.6 fusion.11
  584.3 220.4 %all-to-all-done.2 = bf16[16,12,128,256]{3,2,1,0:T(8,128)(2,1)} async-done(((bf16[16,12,128,256]{3,2,1,0:T(8,128)(2,1)}), bf16[16,12,128,256]{3,2,1,0:T(8,128)(2,1)}, u32[]{:S(2)}, u32[]{:S(2)}) %all-to-all-start.2) | async-done | bytes 12582944 | tf_op jit(solution)/shard_map/all_to_all | solution.py:71
  804.7 12.2 %copy.34 = bf16[24,8,128,256]{3,1,2,0:T(8,128)(2,1)S(1)} copy(bf16[24,8,128,256]{3,2,1,0:T(8,128)(2,1)} %bitcast.29) | data formatting | bytes 25165824
  816.9 5.0 fusion.2
  821.9 7.1 reshape.175
  829.0 22.5 %all-reduce.6.cloned.1.call-done = f32[256,128]{1,0:T(8,128)} async-done(((f32[256,128]{1,0:T(8,128)}), f32[256,128]{1,0:T(8,128)}) %all-reduce.6.cloned.1.call-update) | async-done | bytes 131088 | tf_op jit(solution)/shard_map/psum | solution.py:61
  851.5 1.6 broadcast_multiply_fusion
  853.1 102.1 %reduce-scatter.2.cloned.1.call-done = f32[6144,128]{1,0:T(8,128)} async-done(((f32[6144,256]{1,0:T(8,128)}), f32[6144,128]{1,0:T(8,128)}) %reduce-scatter.2.cloned.1.call-update) | async-done | bytes 3145744 | tf_op jit(solution)/shard_map/reduce_scatter | solution.py:75
  955.2 3.2 convert_element_type.43
  (41 shorter events, 2.1 us)
Async XLA Ops:
  7.2 446.3 %copy-start = (bf16[256,256]{1,0:T(8,128)(2,1)S(1)}, bf16[256,256]{1,0:T(8,128)(2,1)}, u32[]{:S(2)}) copy-start(bf16[256,256]{1,0:T(8,128)(2,1)} %param.8) | copy-start | bytes 393220
  7.2 50.0 %all-gather.3.cloned.1.call-start = ((), (), s32[]{:S(2)}) async-start(), calls=%async_computation.4 | async-start | bytes 4718592 | tf_op jit(solution)/shard_map/all_gather | solution.py:40
  67.2 229.4 %all-to-all-start.1 = ((bf16[16,12,128,256]{3,2,1,0:T(8,128)(2,1)}), bf16[16,12,128,256]{3,2,1,0:T(8,128)(2,1)}, u32[]{:S(2)}, u32[]{:S(2)}) async-start(bf16[16,12,128,256]{3,2,1,0:T(8,128)(2,1)} %bitcast.55), calls=%async_computation.1 | async-start | bytes 25165824 | tf_op jit(solution)/shard_map/all_to_all | solution.py:45
  72.9 380.5 %all-reduce.4.cloned.1.call-start = ((), (), s32[]{:S(2)}) async-start(), calls=%async_computation.5 | async-start | bytes 6291456 | tf_op jit(solution)/shard_map/psum | solution.py:52
  319.7 133.7 %copy-start.3 = (bf16[6144,128]{1,0:T(8,128)(2,1)S(1)}, bf16[6144,128]{1,0:T(8,128)(2,1)}, u32[]{:S(2)}) copy-start(bf16[6144,128]{1,0:T(8,128)(2,1)} %param.9) | copy-start | bytes 4718596
  319.8 184.0 %all-gather.5.cloned.1.call-start = ((), (), s32[]{:S(2)}) async-start(), calls=%async_computation.7 | async-start | bytes 4718592 | tf_op jit(solution)/shard_map/all_gather | solution.py:62
  573.7 7.0 copy-start.2
  573.7 231.0 %all-to-all-start.2 = ((bf16[16,12,128,256]{3,2,1,0:T(8,128)(2,1)}), bf16[16,12,128,256]{3,2,1,0:T(8,128)(2,1)}, u32[]{:S(2)}, u32[]{:S(2)}) async-start(bf16[16,12,128,256]{3,2,1,0:T(8,128)(2,1)} %bitcast.52), calls=%async_computation.2 | async-start | bytes 25165824 | tf_op jit(solution)/shard_map/all_to_all | solution.py:71
  579.3 272.2 %all-reduce.6.cloned.1.call-start = ((), (), s32[]{:S(2)}) async-start(), calls=%async_computation.6 | async-start | bytes 262144 | tf_op jit(solution)/shard_map/psum | solution.py:61
  584.2 371.0 %reduce-scatter.2.cloned.1.call-start = ((), (), s32[]{:S(2)}) async-start(), calls=%async_computation.8 | async-start | bytes 9437184 | tf_op jit(solution)/shard_map/reduce_scatter | solution.py:75
  829.0 129.4 %copy-start.1 = (bf16[256,256]{1,0:T(8,128)(2,1)S(1)}, bf16[256,256]{1,0:T(8,128)(2,1)}, u32[]{:S(2)}) copy-start(bf16[256,256]{1,0:T(8,128)(2,1)} %param.8) | copy-start | bytes 393220
Sparse Core Ops, SparseCore 0:
  9.6 47.5 all-gather.2
  319.9 133.4 all-reduce.3
  458.8 44.8 all-gather.4
  584.4 267.1 all-reduce.5
  853.8 101.3 reduce-scatter.1
where the time goes:
time: 966 us; the launch traced here: 965 us
  waiting for transfers between devices  779 us (81%)
  local copies, waits for them, and re-layouts  103 us (11%)
  matrix products  36.2 us (4%)
  between operations  13.9 us (1%)
  blocking collectives  13.6 us (1%)
  starting transfers between devices  11.7 us (1%)
    all_to_all x1, waiting for transfers between devices, per_device(): lax.all_to_all(served, 'node', split_axis=0, concat_axis=0, tiled=True)  224 us
    all_to_all x1, waiting for transfers between devices, per_device(): lax.all_to_all(outgoing, 'node', split_axis=0, concat_axis=0, tiled=True)  220 us
    psum x1, waiting for transfers between devices, per_device(): lax.psum(partial_value, 'feat').astype(jnp.float32).astype(jnp.bfloat16)  133 us
    reduce_scatter x1, waiting for transfers between devices, per_device(): lax.psum_scatter(owned_sum, 'feat', scatter_dimension=1, tiled=True)  102 us
    all_gather x1, waiting for transfers between devices, per_device(): grad_wide = lax.all_gather(grad_pre, 'feat', axis=1, tiled=True)  45.1 us
    scatter x1, local copies, waits for them, and re-layouts, per_device(): outgoing.at[slot_dest].set(contribution.reshape(-1, tile_size, feat_width))  35.2 us
    all_gather x1, waiting for transfers between devices, per_device(): whole_rows = lax.all_gather(features, 'feat', axis=1, tiled=True)  31 us
    psum x1, waiting for transfers between devices, per_device(): grad_weight = lax.psum(local_weight, 'node') / math.sqrt(nodes_all)  22.5 us
  transfers between devices with their start and end apart: 7, of which 7 were waited for; matrix products, arithmetic and copies ran while one was open for 4% of the time, Pallas kernels for 0%

commit v1 on v0

v1 whole, which is shorter than its diff:
```python
import functools
import math

import jax
import jax.numpy as jnp
from jax import lax
from jax.experimental import pallas as pl
from jax.experimental.pallas import tpu as pltpu
from jax.sharding import PartitionSpec as P

MESH = pl.DeviceIdType.MESH
F32 = jnp.float32
BF16 = jnp.bfloat16


def ring_node(pos, core, depth):
    x = pos // depth
    z = pos * (1 - 2 * x) + x * (2 * depth - 1)
    return (z * 2 + x) * 2 + core


def ring_here(n_node):
    depth = n_node // 4
    me = lax.axis_index("node")
    core, x, z = me % 2, (me // 2) % 2, me // 4
    pos = z * (1 - 2 * x) + x * (2 * depth - 1)
    return me, core, pos, depth


def remote(src, dst, send, recv, node, feat):
    return pltpu.make_async_remote_copy(
        src_ref=src,
        dst_ref=dst,
        send_sem=send,
        recv_sem=recv,
        device_id=(node, feat),
        device_id_type=MESH,
    )


def greet(devices):
    barrier = pltpu.get_barrier_semaphore()
    for node, feat in devices:
        pl.semaphore_signal(barrier, inc=1, device_id=(node, feat), device_id_type=MESH)
    pl.semaphore_wait(barrier, len(devices))


def gather_kernel(
    n_node, feats, tiles, cols, all_feats, all_tiles, all_cols,
    ring_send, ring_recv, core_send, core_recv, own_sem, swap_send, swap_recv,
):
    me, core, pos, depth = ring_here(n_node)
    feat = lax.axis_index("feat")
    count = 2 * depth
    half = feats.shape[0] // 2
    right = ring_node((pos + 1) % count, core, depth)
    left = ring_node((pos + count - 1) % count, core, depth)
    sibling = me + 1 - 2 * core
    greet([(right, feat), (left, feat), (sibling, feat), (me, 1 - feat)])

    pending = []
    parts = swap_send.shape[0] - 1
    rows = tiles.shape[0] // parts
    for i in range(parts):
        piece = pl.ds(i * rows, rows)
        pending.append(
            remote(tiles.at[piece], all_tiles.at[piece], swap_send.at[i], swap_recv.at[i], me, 1 - feat)
        )
    pending.append(remote(cols, all_cols, swap_send.at[parts], swap_recv.at[parts], me, 1 - feat))

    targets = (right, left)
    steps = [[], []]
    for step in range(count - 1):
        for way in range(2):
            at = (pos + count - step) % count if way == 0 else (pos + step) % count
            origin = ring_node(at, core, depth)
            piece = pl.ds(way * half, half)
            src = feats.at[piece] if step == 0 else all_feats.at[origin, piece]
            if step > 0:
                steps[way][step - 1].wait_recv()
            copy = remote(
                src, all_feats.at[origin, piece],
                ring_send.at[way, step], ring_recv.at[way, step], targets[way], feat,
            )
            copy.start()
            steps[way].append(copy)
            share = remote(
                src, all_feats.at[origin, piece],
                core_send.at[way, step], core_recv.at[way, step], sibling, feat,
            )
            share.start()
            pending.append(share)
        if step == 0:
            for swap in pending[: parts + 1]:
                swap.start()
            own = pltpu.make_async_copy(feats, all_feats.at[me], own_sem)
            own.start()
    for way in range(2):
        at = (pos + 1) % count if way == 0 else (pos + count - 1) % count
        origin = ring_node(at, core, depth)
        piece = pl.ds(way * half, half)
        steps[way][count - 2].wait_recv()
        share = remote(
            all_feats.at[origin, piece], all_feats.at[origin, piece],
            core_send.at[way, count - 1], core_recv.at[way, count - 1], sibling, feat,
        )
        share.start()
        pending.append(share)
    own.wait()
    for way in range(2):
        for copy in steps[way]:
            copy.wait_send()
    for copy in pending:
        copy.wait_send()
        copy.wait_recv()


def gather_all(features, tile_vals, block_cols, n_node):
    any_space = pl.BlockSpec(memory_space=pl.ANY)
    count = n_node // 2
    dma = pltpu.SemaphoreType.DMA
    return pl.pallas_call(
        functools.partial(gather_kernel, n_node),
        out_shape=(
            jax.ShapeDtypeStruct((n_node, *features.shape), features.dtype),
            jax.ShapeDtypeStruct(tile_vals.shape, tile_vals.dtype),
            jax.ShapeDtypeStruct(block_cols.shape, block_cols.dtype),
        ),
        in_specs=[any_space] * 3,
        out_specs=[any_space] * 3,
        scratch_shapes=[
            dma((2, count - 1)), dma((2, count - 1)),
            dma((2, count)), dma((2, count)),
            dma, dma((5,)), dma((5,)),
        ],
        compiler_params=pltpu.CompilerParams(
            collective_id=0, has_side_effects=True, vmem_limit_bytes=4 << 20
        ),
        name="gather_ring",
    )(features, tile_vals, block_cols)


def scatter_kernel(
    n_node, part, out, held, own, arrived,
    own_sem, core_send, core_recv, ring_send, ring_recv,
):
    me, core, pos, depth = ring_here(n_node)
    feat = lax.axis_index("feat")
    count = 2 * depth
    half = out.shape[0] // 2
    right = ring_node((pos + 1) % count, core, depth)
    left = ring_node((pos + count - 1) % count, core, depth)
    sibling = me + 1 - 2 * core
    greet([(right, feat), (left, feat), (sibling, feat)])
    targets = (right, left)

    def target_at(way, step):
        back = (pos + 2 * count - 1 - step) % count
        return back if way == 0 else (pos + 1 + step) % count

    shares, loads = {}, {}
    for step in range(count):
        for way in range(2):
            at = target_at(way, step)
            piece = pl.ds(way * half, half)
            copy = remote(
                part.at[ring_node(at, 1 - core, depth), piece], held.at[way, step],
                core_send.at[way, step], core_recv.at[way, step], sibling, feat,
            )
            copy.start()
            shares[way, step] = copy
            load = pltpu.make_async_copy(
                part.at[ring_node(at, core, depth), piece], own.at[way, step], own_sem.at[way, step]
            )
            load.start()
            loads[way, step] = load

    chunk = 256
    sends = {}
    for step in range(count):
        for way in range(2):
            loads[way, step].wait()
            shares[way, step].wait_recv()
            if step > 0:
                sends[way, step - 1].wait_recv()

            @pl.loop(0, half // chunk)
            def _(i, way=way, step=step):
                rows = pl.ds(pl.multiple_of(i * chunk, chunk), chunk)
                total = own[way, step, rows, :].astype(F32) + held[way, step, rows, :].astype(F32)
                if step > 0:
                    total = total + arrived[way, step - 1, rows, :].astype(F32)
                if step == count - 1:
                    spot = pl.ds(pl.multiple_of(way * half + i * chunk, chunk), chunk)
                    out[spot, :] = total.astype(BF16)
                else:
                    own[way, step, rows, :] = total.astype(BF16)

            if step < count - 1:
                copy = remote(
                    own.at[way, step], arrived.at[way, step],
                    ring_send.at[way, step], ring_recv.at[way, step], targets[way], feat,
                )
                copy.start()
                sends[way, step] = copy
    for copy in shares.values():
        copy.wait_send()
    for copy in sends.values():
        copy.wait_send()


def scatter_sum(part, n_node):
    count = n_node // 2
    rows, width = part.shape[1:]
    half = rows // 2
    dma = pltpu.SemaphoreType.DMA
    return pl.pallas_call(
        functools.partial(scatter_kernel, n_node),
        out_shape=jax.ShapeDtypeStruct((rows, width), BF16),
        in_specs=[pl.BlockSpec(memory_space=pl.ANY)],
        out_specs=pl.BlockSpec(memory_space=pltpu.VMEM),
        scratch_shapes=[
            pltpu.VMEM((2, count, half, width), BF16),
            pltpu.VMEM((2, count, half, width), BF16),
            pltpu.VMEM((2, count - 1, half, width), BF16),
            dma((2, count)),
            dma((2, count)), dma((2, count)),
            dma((2, count - 1)), dma((2, count - 1)),
        ],
        compiler_params=pltpu.CompilerParams(
            collective_id=1, has_side_effects=True, vmem_limit_bytes=48 << 20
        ),
        name="scatter_ring",
    )(part)


def spread_kernel(group, cols_a, cols_b, tiles_a, tiles_b, feats, out):
    base = pl.program_id(0) * group
    for r in range(group):
        total = jnp.zeros(out.shape[1:], F32)
        for cols, tiles in ((cols_a, tiles_a), (cols_b, tiles_b)):
            for k in range(tiles.shape[1]):
                total += jnp.dot(
                    tiles[r, k], feats[cols[base + r, k]], preferred_element_type=F32
                )
        out[r] = total.astype(BF16)


def spread(cols_a, cols_b, tiles_a, tiles_b, feats):
    rows, slots, side, _ = tiles_a.shape
    blocks, _, width = feats.shape
    group = math.gcd(rows, 4)
    tile_spec = pl.BlockSpec((group, slots, side, side), lambda i, *_: (i, 0, 0, 0))
    return pl.pallas_call(
        functools.partial(spread_kernel, group),
        out_shape=jax.ShapeDtypeStruct((rows, side, width), BF16),
        grid_spec=pltpu.PrefetchScalarGridSpec(
            num_scalar_prefetch=2,
            grid=(rows // group,),
            in_specs=[
                tile_spec,
                tile_spec,
                pl.BlockSpec((blocks, side, width), lambda i, *_: (0, 0, 0), pipeline_mode=pl.Buffered(1)),
            ],
            out_specs=pl.BlockSpec((group, side, width), lambda i, *_: (i, 0, 0)),
        ),
        compiler_params=pltpu.CompilerParams(vmem_limit_bytes=40 << 20),
        cost_estimate=pl.CostEstimate(
            flops=4 * rows * slots * side * side * width,
            bytes_accessed=2 * (feats.size + 2 * tiles_a.size),
            transcendentals=0,
        ),
        name="spread",
    )(cols_a, cols_b, tiles_a, tiles_b, feats)


def collect_kernel(group, cols_a, cols_b, tiles_a, tiles_b, grads, part):
    @pl.when(pl.program_id(0) == 0)
    def _():
        @pl.loop(0, part.shape[0])
        def _(i):
            part[i] = jnp.zeros(part.shape[1:], BF16)

    base = pl.program_id(0) * group
    for r in range(group):
        for cols, tiles in ((cols_a, tiles_a), (cols_b, tiles_b)):
            for k in range(tiles.shape[1]):
                term = lax.dot_general(
                    tiles[r, k], grads[r], (((0,), (0,)), ((), ())), preferred_element_type=F32
                )
                block = cols[base + r, k]
                part[block] = (part[block].astype(F32) + term).astype(BF16)


def collect(cols_a, cols_b, tiles_a, tiles_b, grads, blocks):
    rows, slots, side, _ = tiles_a.shape
    width = grads.shape[2]
    group = math.gcd(rows, 4)
    tile_spec = pl.BlockSpec((group, slots, side, side), lambda i, *_: (i, 0, 0, 0))
    return pl.pallas_call(
        functools.partial(collect_kernel, group),
        out_shape=jax.ShapeDtypeStruct((blocks, side, width), BF16),
        grid_spec=pltpu.PrefetchScalarGridSpec(
            num_scalar_prefetch=2,
            grid=(rows // group,),
            in_specs=[
                tile_spec,
                tile_spec,
                pl.BlockSpec((group, side, width), lambda i, *_: (i, 0, 0)),
            ],
            out_specs=pl.BlockSpec((blocks, side, width), lambda i, *_: (0, 0, 0), pipeline_mode=pl.Buffered(1)),
        ),
        compiler_params=pltpu.CompilerParams(vmem_limit_bytes=40 << 20),
        cost_estimate=pl.CostEstimate(
            flops=4 * rows * slots * side * side * width,
            bytes_accessed=2 * (blocks * side * width + 2 * tiles_a.size),
            transcendentals=0,
        ),
        name="collect",
    )(cols_a, cols_b, tiles_a, tiles_b, grads)


def per_device_pair(features, block_cols, tile_vals, weight, cotangent):
    n_node = lax.axis_size("node")
    nodes, width = features.shape
    rows = block_cols.shape[0]
    side = tile_vals.shape[2]
    blocks = rows * n_node
    feat = lax.axis_index("feat")
    swap = [(0, 1), (1, 0)]

    def w_block(i, j):
        return lax.dynamic_slice(weight, (i * width, j * width), (width, width))

    def dot(a, b):
        return jnp.dot(a, b, preferred_element_type=F32)

    all_feats, tiles_b, cols_b = gather_all(features, tile_vals, block_cols, n_node)
    agg = spread(
        block_cols, cols_b, tile_vals, tiles_b, all_feats.reshape(blocks, side, width)
    ).reshape(nodes, width)
    agg_b = lax.ppermute(agg, "feat", swap)
    other = 1 - feat
    pre_act = dot(agg, w_block(feat, feat)) + dot(agg_b, w_block(other, feat))
    gate = jax.nn.sigmoid(pre_act)
    activated = (pre_act * gate).astype(BF16)
    grad_pre = (cotangent.astype(F32) * gate * (1.0 + pre_act * (1.0 - gate))).astype(BF16)
    grad_pre_b = lax.ppermute(grad_pre, "feat", swap)
    grad_agg = (
        dot(grad_pre, w_block(feat, feat).T) + dot(grad_pre_b, w_block(feat, other).T)
    ).astype(BF16)
    mine, theirs = dot(agg.T, grad_pre), dot(agg_b.T, grad_pre)
    local = jnp.where(
        feat == 0, jnp.concatenate([mine, theirs]), jnp.concatenate([theirs, mine])
    )
    grad_weight = lax.psum(local, "node") / math.sqrt(nodes * n_node)
    part = collect(
        block_cols, cols_b, tile_vals, tiles_b, grad_agg.reshape(rows, side, width), blocks
    )
    grad_feats = scatter_sum(part.reshape(n_node, nodes, width), n_node)
    return activated, grad_weight, grad_feats


def per_device(features, block_cols, tile_vals, weight, cotangent):
    nodes_dev = lax.axis_size("node")
    rows_blocks = block_cols.shape[0]
    slot_count = block_cols.shape[1]
    tile_size = tile_vals.shape[2]
    feat_width = weight.shape[0]
    col_share = features.shape[1]
    capacity = max(2, (rows_blocks + nodes_dev - 1) // nodes_dev)
    cap_all = slot_count * capacity
    spots = nodes_dev * cap_all
    col_index = lax.axis_index("feat")
    weight_cols = lax.dynamic_slice_in_dim(weight, col_index * col_share, col_share, 1)
    whole_rows = lax.all_gather(features, "feat", axis=1, tiled=True)

    flat = block_cols.reshape(-1)
    entries = jnp.arange(flat.shape[0], dtype=jnp.int32)
    owner = flat // rows_blocks
    earlier = (owner[:, None] == owner[None, :]) & (entries[None, :] < entries[:, None])
    slot_dest = owner * cap_all + jnp.sum(earlier.astype(jnp.int32), axis=1)
    placed = slot_dest[:, None] == jnp.arange(spots, dtype=jnp.int32)[None, :]
    request = jnp.sum(jnp.where(placed, (flat % rows_blocks)[:, None], 0), axis=0)
    placed = placed.astype(BF16)
    wanted = lax.all_to_all(
        request.reshape(nodes_dev, cap_all), "node", split_axis=0, concat_axis=0, tiled=True
    ).reshape(-1)
    selector = (
        wanted[:, None] == jnp.arange(rows_blocks, dtype=jnp.int32)[None, :]
    ).astype(BF16)

    def send(blocks):
        blocks = blocks.reshape(nodes_dev, cap_all, -1)
        got = lax.all_to_all(blocks, "node", split_axis=0, concat_axis=0, tiled=True)
        return got.reshape(spots, -1)

    fetched = send(jnp.dot(selector, whole_rows.reshape(rows_blocks, -1)))
    gathered = jnp.dot(placed, fetched)
    gathered = gathered.reshape(rows_blocks, slot_count, tile_size, feat_width)
    partial_value = jnp.einsum("rsab,rsbf->raf", tile_vals, gathered, preferred_element_type=F32)
    partial_value = partial_value.astype(BF16).reshape(rows_blocks * tile_size, feat_width)
    aggregate = lax.psum(partial_value, "feat").astype(F32).astype(BF16)
    pre_act = jnp.dot(aggregate, weight_cols, preferred_element_type=F32)
    gate_sig = jax.nn.sigmoid(pre_act)
    activated = (pre_act * gate_sig).astype(BF16)
    grad_pre = (
        cotangent.astype(F32) * gate_sig * (1.0 + pre_act * (1.0 - gate_sig))
    ).astype(BF16)
    local_weight = jnp.dot(aggregate.T, grad_pre, preferred_element_type=F32)
    nodes_all = rows_blocks * tile_size * nodes_dev
    grad_weight = lax.psum(local_weight, "node") / math.sqrt(nodes_all)
    grad_wide = lax.all_gather(grad_pre, "feat", axis=1, tiled=True)
    grad_agg = jnp.dot(grad_wide, weight.T, preferred_element_type=F32).astype(BF16)
    grad_agg = grad_agg.reshape(rows_blocks, tile_size, feat_width)
    contribution = jnp.einsum(
        "rsab,raf->rsbf", tile_vals, grad_agg, preferred_element_type=F32
    ).astype(BF16)
    incoming = send(jnp.dot(placed.T, contribution.reshape(flat.shape[0], -1)))
    owned_sum = jnp.dot(selector.T, incoming, preferred_element_type=F32).reshape(
        rows_blocks * tile_size, feat_width
    )
    grad_feats = lax.psum_scatter(owned_sum, "feat", scatter_dimension=1, tiled=True).astype(BF16)
    return (activated, grad_weight, grad_feats)


def solution(mesh):
    pair = mesh.shape["feat"] == 2 and mesh.shape["node"] == 16
    return jax.shard_map(
        per_device_pair if pair else per_device,
        mesh=mesh,
        in_specs=(
            P("node", "feat"),
            P("node", "feat"),
            P("node", "feat", None, None),
            P(),
            P("node", "feat"),
        ),
        out_specs=(P("node", "feat"), P(None, "feat"), P("node", "feat")),
        check_vma=False,
    )
```

time: 966 us -> 483 us (0.50)
  waiting for transfers between devices: 779 us -> 121 us
  Pallas kernels: 0 us -> 313 us
  local copies, waits for them, and re-layouts: 103 us -> 20 us
  matrix products: 36.2 us -> 12.2 us
  blocking collectives: 13.6 us -> 0 us
  starting transfers between devices: 11.7 us -> 1.09 us
    all_to_all x2 -> x0, waiting for transfers between devices: 444 us -> none  [the longest x1 224 us: per_device(): lax.all_to_all(served, 'node', split_axis=0, concat_axis=0, tiled=True)]
    pallas_call x0 -> x4, Pallas kernels: none -> 313 us  [the longest x1 141 us: gather_all(): pl.pallas_call(functools.partial(gather_kernel, n_node), out_shape=(jax.S...]
    reduce_scatter x1 -> x0, waiting for transfers between devices: 102 us -> none  [per_device(): lax.psum_scatter(owned_sum, 'feat', scatter_dimension=1, tiled=True)]
    all_gather x2 -> x0, waiting for transfers between devices: 76 us -> none  [the longest x1 45.1 us: per_device(): grad_wide = lax.all_gather(grad_pre, 'feat', axis=1, tiled=True)]
    psum x2 -> x1, waiting for transfers between devices: 156 us -> 86.3 us  [per_device_pair(): grad_weight = lax.psum(local, 'node') / math.sqrt(nodes * n_node)]
    scatter x2 -> x0, local copies, waits for them, and re-layouts: 36.4 us -> none  [the longest x1 35.2 us: per_device(): outgoing.at[slot_dest].set(contribution.reshape(-1, tile_size, feat_width))]
    ppermute x0 -> x2, waiting for transfers between devices: none -> 34.2 us  [the longest x1 34.2 us: per_device_pair(): agg_b = lax.ppermute(agg, 'feat', swap)]
    dot_general x6, matrix products: 36.2 us -> 12.2 us  [dot(): return jnp.dot(a, b, preferred_element_type=F32)]
  transfers between devices with their start and end apart: 7 -> 3, of which waited for: 7 -> 2; matrix products, arithmetic and copies ran while one was open for 4% -> 2% of each run, Pallas kernels for 0% -> 0%
where the time goes in v1:
time: 483 us
  Pallas kernels  313 us (65%)
  waiting for transfers between devices  121 us (25%)
  local copies, waits for them, and re-layouts  20 us (4%)
  between operations  14.1 us (3%)
  matrix products  12.2 us (3%)
    pallas_call x1, Pallas kernels, gather_all(): pl.pallas_call(functools.partial(gather_kernel, n_node), out_shape=(jax.S...  141 us
    pallas_call x1, Pallas kernels, scatter_sum(): pl.pallas_call(functools.partial(scatter_kernel, n_node), out_shape=jax.S...  136 us
    psum x1, waiting for transfers between devices, per_device_pair(): grad_weight = lax.psum(local, 'node') / math.sqrt(nodes * n_node)  86.3 us
    ppermute x1, waiting for transfers between devices, per_device_pair(): agg_b = lax.ppermute(agg, 'feat', swap)  34.2 us
    pallas_call x1, Pallas kernels, collect(): pl.pallas_call(functools.partial(collect_kernel, group), out_shape=jax.Sh...  20.3 us
    unnamed x22, local copies, waits for them, and re-layouts  20 us
    pallas_call x1, Pallas kernels, spread(): pl.pallas_call(functools.partial(spread_kernel, group), out_shape=jax.Sha...  15.7 us
    dot_general x6, matrix products, dot(): return jnp.dot(a, b, preferred_element_type=F32)  12.2 us
  transfers between devices with their start and end apart: 3, of which 2 were waited for; matrix products, arithmetic and copies ran while one was open for 2% of the time, Pallas kernels for 0%

profile of v1, /device:TPU:0, one launch (start us, length us, event | category | flops | bytes accessed | tf_op | source)
XLA Modules:
  0.0 482.9 jit_solution(1891351875735137569)
XLA Ops:
  7.2 0.0 copy-start
  7.2 0.0 all-reduce.2.cloned.1.call-start
  7.2 0.8 copy.9.cols.cols_a
  8.0 2.8 copy-done.2
  10.8 1.4 copy-done.8
  12.2 141.0 %gather_ring.1 = (bf16[16,6144,128]{2,1,0:T(8,128)(2,1)S(1)}, bf16[48,4,128,128]{3,2,1,0:T(8,128)(2,1)S(1)}, s32[48,4]{1,0:T(8,128)S(1)}) custom-call(bf16[6144,128]{1,0:T(8,128)(2,1)S(1)} %copy-done.8, bf16[48,4,128,128]{3,2,1,0:T(8,128)(2,1)S(1)} %copy-done.2, s32[48,4]{1,0:T(8,128)S(1)} %copy.9.cols.cols_a), custom_call_target="tpu_custom_call" | custom-call | tf_op jit(solution)/shard_map/gather_ring/pallas_call | solution.py:122
  153.2 8.3 %copy-done.5 = bf16[16,6144,128]{2,1,0:T(8,128)(2,1)} copy-done((bf16[16,6144,128]{2,1,0:T(8,128)(2,1)}, bf16[16,6144,128]{2,1,0:T(8,128)(2,1)S(1)}, u32[]{:S(2)}) %copy-start.5) | copy-done | bytes 25165848
  161.5 0.0 copy-done.3
  161.5 15.7 %spread.1 = bf16[48,128,128]{2,1,0:T(8,128)(2,1)S(1)} custom-call(s32[48,4]{1,0:T(8,128)S(1)} %copy.9.cols.cols_a, s32[48,4]{1,0:T(8,128)S(1)} %get-tuple-element.6.cols_b, bf16[48,4,128,128]{3,2,1,0:T(8,128)(2,1)S(1)} %copy-done.3, bf16[48,4,128,128]{3,2,1,0:T(8,128)(2,1)S(1)} %get-tuple-element.7.tiles_b, bf16[768,128,128]{2,1,0:T(8,128)(2,1)} %bitcast.12), custom_call_target="tpu_custom_call" | custom-call | flops 1610612736 | bytes 37748736 | tf_op jit(solution)/shard_map/spread/pallas_call | solution.py:254
  177.2 0.0 copy-done.6
  177.2 0.6 collective-permute-start
  177.8 0.6 fusion.5
  178.3 34.2 %collective-permute-done = bf16[6144,128]{1,0:T(8,128)(2,1)S(1)} collective-permute-done((bf16[6144,128]{1,0:T(8,128)(2,1)S(1)}, bf16[6144,128]{1,0:T(8,128)(2,1)S(1)}, u32[]{:S(2)}, u32[]{:S(2)}) %collective-permute-start) | collective-permute-done | bytes 1572896 | tf_op jit(solution)/shard_map/ppermute | solution.py:342
  212.5 3.6 multiply_convert_fusion
  216.2 0.5 collective-permute-start.1
  216.7 2.1 fusion.7
  218.7 2.0 fusion.8
  220.7 0.7 maximum_select_fusion
  221.4 0.0 all-reduce.2.cloned.1.call-update
  221.4 2.0 fusion.3
  223.4 86.3 %all-reduce.2.cloned.1.call-done = f32[256,128]{1,0:T(8,128)} async-done(((f32[256,128]{1,0:T(8,128)}), f32[256,128]{1,0:T(8,128)}) %all-reduce.2.cloned.1.call-update) | async-done | bytes 131088 | tf_op jit(solution)/shard_map/psum | solution.py:356
  309.7 1.6 broadcast_multiply_fusion
  311.3 0.0 collective-permute-done.1
  311.3 2.0 fusion
  313.3 0.0 copy-start.4
  313.3 2.8 copy-done.4
  316.1 2.8 copy-done.7
  318.8 20.3 %collect.1 = bf16[768,128,128]{2,1,0:T(8,128)(2,1)} custom-call(s32[48,4]{1,0:T(8,128)S(1)} %copy.9.cols.cols_a, s32[48,4]{1,0:T(8,128)S(1)} %get-tuple-element.6.cols_b, bf16[48,4,128,128]{3,2,1,0:T(8,128)(2,1)S(1)} %copy-done.4, bf16[48,4,128,128]{3,2,1,0:T(8,128)(2,1)S(1)} %copy-done.7, bf16[48,128,128]{2,1,0:T(8,128)(2,1)S(1)} %bitcast.16), custom_call_target="tpu_custom_call" | custom-call | flops 1610612736 | bytes 37748736 | tf_op jit(solution)/shard_map/collect/pallas_call | solution.py:300
  339.1 135.8 %scatter_ring.1 = bf16[6144,128]{1,0:T(8,128)(2,1)S(1)} custom-call(bf16[16,6144,128]{2,1,0:T(8,128)(2,1)} %bitcast.17), custom_call_target="tpu_custom_call" | custom-call | tf_op jit(solution)/shard_map/scatter_ring/pallas_call | solution.py:217
  474.9 0.0 copy-start.1
  474.9 1.1 copy.13
  476.1 0.0 copy-done.1
  (9 shorter events, 0.0 us)
Async XLA Ops:
  7.2 170.6 %copy-start = (bf16[256,256]{1,0:T(8,128)(2,1)S(1)}, bf16[256,256]{1,0:T(8,128)(2,1)}, u32[]{:S(2)}) copy-start(bf16[256,256]{1,0:T(8,128)(2,1)} %param.8) | copy-start | bytes 393220
  7.2 302.5 %all-reduce.2.cloned.1.call-start = ((), (), s32[]{:S(2)}) async-start(), calls=%async_computation | async-start | bytes 262144 | tf_op jit(solution)/shard_map/psum | solution.py:356
  8.0 2.8 copy-start.2
  10.8 1.4 copy-start.8
  12.2 149.3 %copy-start.3 = (bf16[48,4,128,128]{3,2,1,0:T(8,128)(2,1)S(1)}, bf16[48,4,128,128]{3,2,1,0:T(8,128)(2,1)}, u32[]{:S(2)}) copy-start(bf16[48,4,128,128]{3,2,1,0:T(8,128)(2,1)} %tiles_a.3) | copy-start | bytes 18874372
  153.2 8.3 %copy-start.5 = (bf16[16,6144,128]{2,1,0:T(8,128)(2,1)}, bf16[16,6144,128]{2,1,0:T(8,128)(2,1)S(1)}, u32[]{:S(2)}) copy-start(bf16[16,6144,128]{2,1,0:T(8,128)(2,1)S(1)} %get-tuple-element.8) | copy-start | bytes 75497472
  161.5 15.7 %copy-start.6 = (bf16[48,4,128,128]{3,2,1,0:T(8,128)(2,1)}, bf16[48,4,128,128]{3,2,1,0:T(8,128)(2,1)S(1)}, u32[]{:S(2)}) copy-start(bf16[48,4,128,128]{3,2,1,0:T(8,128)(2,1)S(1)} %get-tuple-element.7.tiles_b) | copy-start | bytes 18874372
  177.2 35.3 %collective-permute-start = (bf16[6144,128]{1,0:T(8,128)(2,1)S(1)}, bf16[6144,128]{1,0:T(8,128)(2,1)S(1)}, u32[]{:S(2)}, u32[]{:S(2)}) collective-permute-start(bf16[6144,128]{1,0:T(8,128)(2,1)S(1)} %bitcast.13), channel_id=1, source_target_pairs={{0,1},{1,0},{2,3},{3,2},{4,5},{5,4},{6,7},{7,6},{8,9},{9,8},{10,11... | collective-permute-start | bytes 4718600 | tf_op jit(solution)/shard_map/ppermute | solution.py:342
  177.8 34.8 %copy-start.9 = (bf16[6144,128]{1,0:T(8,128)(2,1)S(1)}, bf16[6144,128]{1,0:T(8,128)(2,1)}, u32[]{:S(2)}) copy-start(bf16[6144,128]{1,0:T(8,128)(2,1)} %param.9) | copy-start | bytes 4718596
  216.2 95.1 %collective-permute-start.1 = (bf16[6144,128]{1,0:T(8,128)(2,1)}, bf16[6144,128]{1,0:T(8,128)(2,1)}, u32[]{:S(2)}, u32[]{:S(2)}) collective-permute-start(bf16[6144,128]{1,0:T(8,128)(2,1)} %get-tuple-element.9), channel_id=1, source_target_pairs={{0,1},{1,0},{2,3},{3,2},{4,5},{5,4},{6,7},{7,6},{8,9},{9,8},{10,11... | collective-permute-start | bytes 4718600 | tf_op jit(solution)/shard_map/ppermute | solution.py:348
  313.3 2.8 copy-start.4
  316.1 2.8 copy-start.7
  474.9 1.2 copy-start.1
Sparse Core Ops, SparseCore 0:
  221.5 88.1 all-reduce.1

commit v2 on v1

--- a/solution.py
+++ b/solution.py
@@ -11,6 +11,7 @@
 MESH = pl.DeviceIdType.MESH
 F32 = jnp.float32
 BF16 = jnp.bfloat16
+STREAMS = 4
 
 
 def ring_node(pos, core, depth):
@@ -52,7 +53,7 @@
     me, core, pos, depth = ring_here(n_node)
     feat = lax.axis_index("feat")
     count = 2 * depth
-    half = feats.shape[0] // 2
+    size = feats.shape[0] // STREAMS
     right = ring_node((pos + 1) % count, core, depth)
     left = ring_node((pos + count - 1) % count, core, depth)
     sibling = me + 1 - 2 * core
@@ -69,25 +70,24 @@
     pending.append(remote(cols, all_cols, swap_send.at[parts], swap_recv.at[parts], me, 1 - feat))
 
     targets = (right, left)
-    steps = [[], []]
-    for step in range(count - 1):
-        for way in range(2):
+    steps = {}
+    for step in range(count):
+        for j in range(STREAMS):
+            way = j % 2
             at = (pos + count - step) % count if way == 0 else (pos + step) % count
             origin = ring_node(at, core, depth)
-            piece = pl.ds(way * half, half)
-            src = feats.at[piece] if step == 0 else all_feats.at[origin, piece]
+            piece = pl.ds(j * size, size)
+            dst = all_feats.at[origin, piece]
+            src = feats.at[piece] if step == 0 else dst
             if step > 0:
-                steps[way][step - 1].wait_recv()
-            copy = remote(
-                src, all_feats.at[origin, piece],
-                ring_send.at[way, step], ring_recv.at[way, step], targets[way], feat,
-            )
-            copy.start()
-            steps[way].append(copy)
-            share = remote(
-                src, all_feats.at[origin, piece],
-                core_send.at[way, step], core_recv.at[way, step], sibling, feat,
-            )
+                steps[j, step - 1].wait_recv()
+            if step < count - 1:
+                copy = remote(
+                    src, dst, ring_send.at[j, step], ring_recv.at[j, step], targets[way], feat
+                )
+                copy.start()
+                steps[j, step] = copy
+            share = remote(src, dst, core_send.at[j, step], core_recv.at[j, step], sibling, feat)
             share.start()
             pending.append(share)
         if step == 0:
@@ -95,21 +95,9 @@
                 swap.start()
             own = pltpu.make_async_copy(feats, all_feats.at[me], own_sem)
             own.start()
-    for way in range(2):
-        at = (pos + 1) % count if way == 0 else (pos + count - 1) % count
-        origin = ring_node(at, core, depth)
-        piece = pl.ds(way * half, half)
-        steps[way][count - 2].wait_recv()
-        share = remote(
-            all_feats.at[origin, piece], all_feats.at[origin, piece],
-            core_send.at[way, count - 1], core_recv.at[way, count - 1], sibling, feat,
-        )
-        share.start()
-        pending.append(share)
     own.wait()
-    for way in range(2):
-        for copy in steps[way]:
-            copy.wait_send()
+    for copy in steps.values():
+        copy.wait_send()
     for copy in pending:
         copy.wait_send()
         copy.wait_recv()
@@ -129,8 +117,8 @@
         in_specs=[any_space] * 3,
         out_specs=[any_space] * 3,
         scratch_shapes=[
-            dma((2, count - 1)), dma((2, count - 1)),
-            dma((2, count)), dma((2, count)),
+            dma((STREAMS, count - 1)), dma((STREAMS, count - 1)),
+            dma((STREAMS, count)), dma((STREAMS, count)),
             dma, dma((5,)), dma((5,)),
         ],
         compiler_params=pltpu.CompilerParams(
@@ -141,97 +129,145 @@
 
 
 def scatter_kernel(
-    n_node, part, out, held, own, arrived,
+    n_node, scale, part, weight_part, out, weight_out,
+    held, own, arrived, w_sib, w_slots, w_send, w_recv,
     own_sem, core_send, core_recv, ring_send, ring_recv,
 ):
     me, core, pos, depth = ring_here(n_node)
     feat = lax.axis_index("feat")
     count = 2 * depth
-    half = out.shape[0] // 2
+    size = out.shape[0] // STREAMS
     right = ring_node((pos + 1) % count, core, depth)
     left = ring_node((pos + count - 1) % count, core, depth)
     sibling = me + 1 - 2 * core
     greet([(right, feat), (left, feat), (sibling, feat)])
     targets = (right, left)
+    streams = [(j % 2, j) for j in range(STREAMS)]
 
     def target_at(way, step):
         back = (pos + 2 * count - 1 - step) % count
         return back if way == 0 else (pos + 1 + step) % count
 
-    shares, loads = {}, {}
-    for step in range(count):
-        for way in range(2):
+    shares, loads, sends = {}, {}, {}
+
+    def fetch(step):
+        for way, j in streams:
             at = target_at(way, step)
-            piece = pl.ds(way * half, half)
+            piece = pl.ds(j * size, size)
             copy = remote(
-                part.at[ring_node(at, 1 - core, depth), piece], held.at[way, step],
-                core_send.at[way, step], core_recv.at[way, step], sibling, feat,
+                part.at[ring_node(at, 1 - core, depth), piece], held.at[j, step],
+                core_send.at[j, step], core_recv.at[j, step], sibling, feat,
             )
             copy.start()
-            shares[way, step] = copy
+            shares[j, step] = copy
             load = pltpu.make_async_copy(
-                part.at[ring_node(at, core, depth), piece], own.at[way, step], own_sem.at[way, step]
+                part.at[ring_node(at, core, depth), piece], own.at[j, step], own_sem.at[j, step]
             )
             load.start()
-            loads[way, step] = load
-
+            loads[j, step] = load
+
+    w_rows = weight_part.shape[0] // 2
+    w_mine = pl.ds(pl.multiple_of(core * w_rows, w_rows), w_rows)
+    w_theirs = pl.ds(pl.multiple_of((1 - core) * w_rows, w_rows), w_rows)
+    w_copies = []
+
+    def w_copy(src, dst, node):
+        i = len(w_copies)
+        copy = remote(src, dst, w_send.at[i], w_recv.at[i], node, feat)
+        copy.start()
+        w_copies.append(copy)
+        return copy
+
+    w_ways = [[], []]
+    w_lengths = (count // 2, count - 1 - count // 2)
+
+    def weight_step(step):
+        if step == 1:
+            w_copies[0].wait_recv()
+            w_slots[pos] = weight_part[w_mine, :] + w_sib[...]
+        hop = step - 1
+        for way in range(2):
+            if 0 < hop <= w_lengths[way]:
+                w_ways[way][hop - 1].wait_recv()
+            if 0 <= hop < w_lengths[way]:
+                at = (pos + count - hop) % count if way == 0 else (pos + hop) % count
+                w_ways[way].append(w_copy(w_slots.at[at], w_slots.at[at], targets[way]))
+        if hop == count // 2:
+            total = w_slots[0]
+            for i in range(1, count):
+                total = total + w_slots[i]
+            weight_out[w_mine, :] = total * scale
+            w_copy(weight_out.at[w_mine], weight_out.at[w_mine], sibling)
+
+    fetch(0)
+    fetch(1)
+    w_copy(weight_part.at[w_theirs], w_sib, sibling)
     chunk = 256
-    sends = {}
     for step in range(count):
-        for way in range(2):
-            loads[way, step].wait()
-            shares[way, step].wait_recv()
+        for way, j in streams:
+            loads[j, step].wait()
+            shares[j, step].wait_recv()
             if step > 0:
-                sends[way, step - 1].wait_recv()
-
-            @pl.loop(0, half // chunk)
-            def _(i, way=way, step=step):
+                sends[j, step - 1].wait_recv()
+
+            @pl.loop(0, size // chunk)
+            def _(i, j=j, step=step):
                 rows = pl.ds(pl.multiple_of(i * chunk, chunk), chunk)
-                total = own[way, step, rows, :].astype(F32) + held[way, step, rows, :].astype(F32)
+                total = own[j, step, rows, :].astype(F32) + held[j, step, rows, :].astype(F32)
                 if step > 0:
-                    total = total + arrived[way, step - 1, rows, :].astype(F32)
+                    total = total + arrived[j, step - 1, rows, :].astype(F32)
                 if step == count - 1:
-                    spot = pl.ds(pl.multiple_of(way * half + i * chunk, chunk), chunk)
+                    spot = pl.ds(pl.multiple_of(j * size + i * chunk, chunk), chunk)
                     out[spot, :] = total.astype(BF16)
                 else:
-                    own[way, step, rows, :] = total.astype(BF16)
+                    own[j, step, rows, :] = total.astype(BF16)
 
             if step < count - 1:
                 copy = remote(
-                    own.at[way, step], arrived.at[way, step],
-                    ring_send.at[way, step], ring_recv.at[way, step], targets[way], feat,
+                    own.at[j, step], arrived.at[j, step],
+                    ring_send.at[j, step], ring_recv.at[j, step], targets[way], feat,
                 )
                 copy.start()
-                sends[way, step] = copy
-    for copy in shares.values():
+                sends[j, step] = copy
+        if step + 2 < count:
+            fetch(step + 2)
+        weight_step(step)
+    w_copies[-1].wait_recv()
+    for copy in (*shares.values(), *sends.values(), *w_copies):
         copy.wait_send()
-    for copy in sends.values():
-        copy.wait_send()
-
-
-def scatter_sum(part, n_node):
+
+
+def scatter_sum(part, weight_part, scale, n_node):
     count = n_node // 2
     rows, width = part.shape[1:]
-    half = rows // 2
+    size = rows // STREAMS
+    w_rows = weight_part.shape[0] // 2
     dma = pltpu.SemaphoreType.DMA
+    vmem = pl.BlockSpec(memory_space=pltpu.VMEM)
     return pl.pallas_call(
-        functools.partial(scatter_kernel, n_node),
-        out_shape=jax.ShapeDtypeStruct((rows, width), BF16),
-        in_specs=[pl.BlockSpec(memory_space=pl.ANY)],
-        out_specs=pl.BlockSpec(memory_space=pltpu.VMEM),
+        functools.partial(scatter_kernel, n_node, scale),
+        out_shape=(
+            jax.ShapeDtypeStruct((rows, width), BF16),
+            jax.ShapeDtypeStruct(weight_part.shape, F32),
+        ),
+        in_specs=[pl.BlockSpec(memory_space=pl.ANY), vmem],
+        out_specs=(vmem, vmem),
         scratch_shapes=[
-            pltpu.VMEM((2, count, half, width), BF16),
-            pltpu.VMEM((2, count, half, width), BF16),
-            pltpu.VMEM((2, count - 1, half, width), BF16),
-            dma((2, count)),
-            dma((2, count)), dma((2, count)),
-            dma((2, count - 1)), dma((2, count - 1)),
+            pltpu.VMEM((STREAMS, count, size, width), BF16),
+            pltpu.VMEM((STREAMS, count, size, width), BF16),
+            pltpu.VMEM((STREAMS, count - 1, size, width), BF16),
+            pltpu.VMEM((w_rows, width), F32),
+            pltpu.VMEM((count, w_rows, width), F32),
+            dma((count + 1,)), dma((count + 1,)),
+            dma((STREAMS, count)),
+            dma((STREAMS, count)), dma((STREAMS, count)),
+            dma((STREAMS, count - 1)), dma((STREAMS, count - 1)),
         ],
         compiler_params=pltpu.CompilerParams(
             collective_id=1, has_side_effects=True, vmem_limit_bytes=48 << 20
         ),
         name="scatter_ring",
-    )(part)
+    )(part, weight_part)
 
 
 def spread_kernel(group, cols_a, cols_b, tiles_a, tiles_b, feats, out):
@@ -264,7 +300,7 @@
             ],
             out_specs=pl.BlockSpec((group, side, width), lambda i, *_: (i, 0, 0)),
         ),
-        compiler_params=pltpu.CompilerParams(vmem_limit_bytes=40 << 20),
+        compiler_params=pltpu.CompilerParams(vmem_limit_bytes=60 << 20),
         cost_estimate=pl.CostEstimate(
             flops=4 * rows * slots * side * side * width,
             bytes_accessed=2 * (feats.size + 2 * tiles_a.size),
@@ -310,7 +346,7 @@
             ],
             out_specs=pl.BlockSpec((blocks, side, width), lambda i, *_: (0, 0, 0), pipeline_mode=pl.Buffered(1)),
         ),
-        compiler_params=pltpu.CompilerParams(vmem_limit_bytes=40 << 20),
+        compiler_params=pltpu.CompilerParams(vmem_limit_bytes=60 << 20),
         cost_estimate=pl.CostEstimate(
             flops=4 * rows * slots * side * side * width,
             bytes_accessed=2 * (blocks * side * width + 2 * tiles_a.size),
@@ -353,11 +389,12 @@
     local = jnp.where(
         feat == 0, jnp.concatenate([mine, theirs]), jnp.concatenate([theirs, mine])
     )
-    grad_weight = lax.psum(local, "node") / math.sqrt(nodes * n_node)
     part = collect(
         block_cols, cols_b, tile_vals, tiles_b, grad_agg.reshape(rows, side, width), blocks
     )
-    grad_feats = scatter_sum(part.reshape(n_node, nodes, width), n_node)
+    grad_feats, grad_weight = scatter_sum(
+        part.reshape(n_node, nodes, width), local, 1.0 / math.sqrt(nodes * n_node), n_node
+    )
     return activated, grad_weight, grad_feats
 
 

time: 483 us -> 416 us (0.86)
  waiting for transfers between devices: 121 us -> 63.7 us
  between operations: 14.1 us -> 0.72 us
  Pallas kernels: 313 us -> 318 us
    psum x1 -> x0, waiting for transfers between devices: 86.3 us -> none  [per_device_pair(): grad_weight = lax.psum(local, 'node') / math.sqrt(nodes * n_node)]
    ppermute x1, waiting for transfers between devices: 0.01 us -> 30.7 us  [per_device_pair(): grad_pre_b = lax.ppermute(grad_pre, 'feat', swap)]
    pallas_call x1, Pallas kernels: 20.3 us -> 25.4 us  [collect(): pl.pallas_call(functools.partial(collect_kernel, group), out_shape=jax.Sh...]
    pallas_call x1, Pallas kernels: 15.7 us -> 20.6 us  [spread(): pl.pallas_call(functools.partial(spread_kernel, group), out_shape=jax.Sha...]
    pallas_call x1, Pallas kernels: 136 us -> 131 us  [scatter_sum(): pl.pallas_call(functools.partial(scatter_kernel, n_node, scale), out_shap...]
    unnamed x22 -> x23, local copies, waits for them, and re-layouts: 20 us -> 18.4 us
  transfers between devices with their start and end apart: 3 -> 2, of which waited for: 2 -> 2; matrix products, arithmetic and copies ran while one was open for 2% -> 1% of each run, Pallas kernels for 0% -> 0%
where the time goes in v2:
time: 416 us; the launch traced here: 415 us
  Pallas kernels  318 us (76%)
  waiting for transfers between devices  63.7 us (15%)
  local copies, waits for them, and re-layouts  18.4 us (4%)
  matrix products  13 us (3%)
    pallas_call x1, Pallas kernels, gather_all(): pl.pallas_call(functools.partial(gather_kernel, n_node), out_shape=(jax.S...  142 us
    pallas_call x1, Pallas kernels, scatter_sum(): pl.pallas_call(functools.partial(scatter_kernel, n_node, scale), out_shap...  131 us
    ppermute x1, waiting for transfers between devices, per_device_pair(): agg_b = lax.ppermute(agg, 'feat', swap)  33 us
    ppermute x1, waiting for transfers between devices, per_device_pair(): grad_pre_b = lax.ppermute(grad_pre, 'feat', swap)  30.7 us
    pallas_call x1, Pallas kernels, collect(): pl.pallas_call(functools.partial(collect_kernel, group), out_shape=jax.Sh...  25.4 us
    pallas_call x1, Pallas kernels, spread(): pl.pallas_call(functools.partial(spread_kernel, group), out_shape=jax.Sha...  20.6 us
    unnamed x23, local copies, waits for them, and re-layouts  18.4 us
    dot_general x6, matrix products, dot(): return jnp.dot(a, b, preferred_element_type=F32)  13 us
  transfers between devices with their start and end apart: 2, of which 2 were waited for; matrix products, arithmetic and copies ran while one was open for 1% of the time, Pallas kernels for 0%

profile of v2, /device:TPU:0, one launch (start us, length us, event | category | flops | bytes accessed | tf_op | source)
XLA Modules:
  0.0 415.3 jit_solution(4754465299318083619)
XLA Ops:
  0.6 0.0 copy-start
  0.6 0.8 copy.9.cols.cols_a
  1.4 0.0 copy-start.2
  1.5 2.8 copy-done.2
  4.2 1.4 copy-done.5
  5.6 141.6 %gather_ring.1 = (bf16[16,6144,128]{2,1,0:T(8,128)(2,1)S(1)}, bf16[48,4,128,128]{3,2,1,0:T(8,128)(2,1)S(1)}, s32[48,4]{1,0:T(8,128)S(1)}) custom-call(bf16[6144,128]{1,0:T(8,128)(2,1)S(1)} %copy-done.5, bf16[48,4,128,128]{3,2,1,0:T(8,128)(2,1)S(1)} %copy-done.2, s32[48,4]{1,0:T(8,128)S(1)} %copy.9.cols.cols_a), custom_call_target="tpu_custom_call" | custom-call | tf_op jit(solution)/shard_map/gather_ring/pallas_call | solution.py:110
  147.2 0.0 copy-done.6
  147.2 0.0 copy-start.3
  147.2 8.3 %copy-done.3 = bf16[16,6144,128]{2,1,0:T(8,128)(2,1)} copy-done((bf16[16,6144,128]{2,1,0:T(8,128)(2,1)}, bf16[16,6144,128]{2,1,0:T(8,128)(2,1)S(1)}, u32[]{:S(2)}) %copy-start.3) | copy-done | bytes 25165848
  155.5 2.7 copy-done.4
  158.2 0.6 copy-done.7
  158.8 20.6 %spread.1 = bf16[48,128,128]{2,1,0:T(8,128)(2,1)} custom-call(s32[48,4]{1,0:T(8,128)} %copy-done.6, s32[48,4]{1,0:T(8,128)} %copy-done.7, bf16[48,4,128,128]{3,2,1,0:T(8,128)(2,1)} %tiles_a.3, bf16[48,4,128,128]{3,2,1,0:T(8,128)(2,1)} %copy-done.4, bf16[768,128,128]{2,1,0:T(8,128)(2,1)} %bitcast.12), custom_call_target="tpu_custom_call" | custom-call | flops 1610612736 | bytes 37748736 | tf_op jit(solution)/shard_map/spread/pallas_call | solution.py:290
  179.4 0.5 collective-permute-start
  179.9 0.0 copy-done
  179.9 2.1 fusion.5
  182.0 0.0 copy-start.8
  182.0 33.0 %collective-permute-done = bf16[6144,128]{1,0:T(8,128)(2,1)} collective-permute-done((bf16[6144,128]{1,0:T(8,128)(2,1)}, bf16[6144,128]{1,0:T(8,128)(2,1)}, u32[]{:S(2)}, u32[]{:S(2)}) %collective-permute-start) | collective-permute-done | bytes 1572896 | tf_op jit(solution)/shard_map/ppermute | solution.py:378
  215.0 0.0 copy-done.9
  215.0 4.5 %multiply_convert_fusion = (bf16[6144,128]{1,0:T(8,128)(2,1)S(1)}, bf16[6144,128]{1,0:T(8,128)(2,1)}) fusion(bf16[6144,128]{1,0:T(8,128)(2,1)S(1)} %copy-done.9, f32[6144,128]{1,0:T(8,128)S(1)} %fusion.5, bf16[6144,128]{1,0:T(8,128)(2,1)} %collective-permute-done, bf16[256,256]{1,0:T(8,128)(2,1)S(1)} %copy-done, s32[]{:T(128)S(6)} %select_n.21, s32[]{:T(128)S(6)} %select_n.20), kind=kOutput, calls=%fused_computation.3 | convolution fusion | flops 211550208 | bytes 9469960 | tf_op jit(solution)/shard_map/dot_general | solution.py:372
  219.5 0.5 collective-permute-start.1
  220.0 0.0 copy-done.8
  220.0 0.6 fusion.7
  220.6 2.0 fusion.8
  222.7 0.6 fusion.3
  223.2 30.7 %collective-permute-done.1 = bf16[6144,128]{1,0:T(8,128)(2,1)} collective-permute-done((bf16[6144,128]{1,0:T(8,128)(2,1)S(1)}, bf16[6144,128]{1,0:T(8,128)(2,1)}, u32[]{:S(2)}, u32[]{:S(2)}) %collective-permute-start.1) | collective-permute-done | bytes 1572896 | tf_op jit(solution)/shard_map/ppermute | solution.py:384
  253.9 3.2 fusion
  257.1 25.4 %collect.1 = bf16[768,128,128]{2,1,0:T(8,128)(2,1)} custom-call(s32[48,4]{1,0:T(8,128)} %copy-done.6, s32[48,4]{1,0:T(8,128)} %copy-done.7, bf16[48,4,128,128]{3,2,1,0:T(8,128)(2,1)} %tiles_a.3, bf16[48,4,128,128]{3,2,1,0:T(8,128)(2,1)} %copy-done.4, bf16[48,128,128]{2,1,0:T(8,128)(2,1)} %bitcast.17), custom_call_target="tpu_custom_call" | custom-call | flops 1610612736 | bytes 37748736 | tf_op jit(solution)/shard_map/collect/pallas_call | solution.py:336
  282.5 130.9 %scatter_ring.1 = (bf16[6144,128]{1,0:T(8,128)(2,1)S(1)}, f32[256,128]{1,0:T(8,128)S(1)}) custom-call(bf16[16,6144,128]{2,1,0:T(8,128)(2,1)} %bitcast.13, f32[256,128]{1,0:T(8,128)S(1)} %maximum_select_fusion.weight_part), custom_call_target="tpu_custom_call" | custom-call | tf_op jit(solution)/shard_map/scatter_ring/pallas_call | solution.py:247
  413.5 0.0 copy-start.1
  413.5 0.7 copy.13
  414.1 1.1 copy.14
  415.3 0.0 copy-done.1
  (6 shorter events, 0.0 us)
Async XLA Ops:
  0.6 179.3 %copy-start = (bf16[256,256]{1,0:T(8,128)(2,1)S(1)}, bf16[256,256]{1,0:T(8,128)(2,1)}, u32[]{:S(2)}) copy-start(bf16[256,256]{1,0:T(8,128)(2,1)} %param.8) | copy-start | bytes 393220
  1.4 2.8 copy-start.2
  4.2 1.4 copy-start.5
  5.6 141.6 %copy-start.6 = (s32[48,4]{1,0:T(8,128)}, s32[48,4]{1,0:T(8,128)S(1)}, u32[]{:S(2)}) copy-start(s32[48,4]{1,0:T(8,128)S(1)} %copy.9.cols.cols_a) | copy-start | bytes 2308
  147.2 8.3 %copy-start.3 = (bf16[16,6144,128]{2,1,0:T(8,128)(2,1)}, bf16[16,6144,128]{2,1,0:T(8,128)(2,1)S(1)}, u32[]{:S(2)}) copy-start(bf16[16,6144,128]{2,1,0:T(8,128)(2,1)S(1)} %get-tuple-element.10) | copy-start | bytes 75497472
  155.5 2.7 copy-start.4
  158.2 0.6 copy-start.7
  179.4 35.6 %collective-permute-start = (bf16[6144,128]{1,0:T(8,128)(2,1)}, bf16[6144,128]{1,0:T(8,128)(2,1)}, u32[]{:S(2)}, u32[]{:S(2)}) collective-permute-start(bf16[6144,128]{1,0:T(8,128)(2,1)} %bitcast.14), channel_id=1, source_target_pairs={{0,1},{1,0},{2,3},{3,2},{4,5},{5,4},{6,7},{7,6},{8,9},{9,8},{10,11... | collective-permute-start | bytes 4718600 | tf_op jit(solution)/shard_map/ppermute | solution.py:378
  179.9 35.1 %copy-start.9 = (bf16[6144,128]{1,0:T(8,128)(2,1)S(1)}, bf16[6144,128]{1,0:T(8,128)(2,1)}, u32[]{:S(2)}) copy-start(bf16[6144,128]{1,0:T(8,128)(2,1)} %param.9) | copy-start | bytes 4718596
  182.0 38.0 %copy-start.8 = (bf16[48,128,128]{2,1,0:T(8,128)(2,1)S(1)}, bf16[48,128,128]{2,1,0:T(8,128)(2,1)}, u32[]{:S(2)}) copy-start(bf16[48,128,128]{2,1,0:T(8,128)(2,1)} %spread.1) | copy-start | bytes 4718596
  219.5 34.4 %collective-permute-start.1 = (bf16[6144,128]{1,0:T(8,128)(2,1)S(1)}, bf16[6144,128]{1,0:T(8,128)(2,1)}, u32[]{:S(2)}, u32[]{:S(2)}) collective-permute-start(bf16[6144,128]{1,0:T(8,128)(2,1)S(1)} %get-tuple-element.13), channel_id=1, source_target_pairs={{0,1},{1,0},{2,3},{3,2},{4,5},{5,4},{6,7},{7,6},{8,9},{9,8},{10,11... | collective-permute-start | bytes 4718600 | tf_op jit(solution)/shard_map/ppermute | solution.py:384
  413.5 1.8 copy-start.1

commit v3 on v2

--- a/solution.py
+++ b/solution.py
@@ -47,38 +47,38 @@
 
 
 def gather_kernel(
-    n_node, feats, tiles, cols, all_feats, all_tiles, all_cols,
+    n_node, feats, tiles, cols, cols_here, agg, agg_b, all_tiles, all_cols,
+    held, tiles_a, tiles_b, cols_b, total,
     ring_send, ring_recv, core_send, core_recv, own_sem, swap_send, swap_recv,
+    agg_send, agg_recv, keep_sem,
 ):
     me, core, pos, depth = ring_here(n_node)
     feat = lax.axis_index("feat")
     count = 2 * depth
-    size = feats.shape[0] // STREAMS
+    rows = feats.shape[0]
+    size = rows // STREAMS
     right = ring_node((pos + 1) % count, core, depth)
     left = ring_node((pos + count - 1) % count, core, depth)
     sibling = me + 1 - 2 * core
     greet([(right, feat), (left, feat), (sibling, feat), (me, 1 - feat)])
 
-    pending = []
     parts = swap_send.shape[0] - 1
-    rows = tiles.shape[0] // parts
+    swaps = []
     for i in range(parts):
-        piece = pl.ds(i * rows, rows)
-        pending.append(
-            remote(tiles.at[piece], all_tiles.at[piece], swap_send.at[i], swap_recv.at[i], me, 1 - feat)
+        piece = pl.ds(i * (rows // parts), rows // parts)
+        swaps.append(
+            remote(tiles.at[piece], tiles_b.at[piece], swap_send.at[i], swap_recv.at[i], me, 1 - feat)
         )
-    pending.append(remote(cols, all_cols, swap_send.at[parts], swap_recv.at[parts], me, 1 - feat))
+    swaps.append(remote(cols, all_cols, swap_send.at[parts], swap_recv.at[parts], me, 1 - feat))
 
     targets = (right, left)
-    steps = {}
+    steps, shares = {}, []
     for step in range(count):
         for j in range(STREAMS):
             way = j % 2
             at = (pos + count - step) % count if way == 0 else (pos + step) % count
-            origin = ring_node(at, core, depth)
-            piece = pl.ds(j * size, size)
-            dst = all_feats.at[origin, piece]
-            src = feats.at[piece] if step == 0 else dst
+            dst = held.at[pl.ds(ring_node(at, core, depth) * rows + j * size, size)]
+            src = feats.at[pl.ds(j * size, size)] if step == 0 else dst
             if step > 0:
                 steps[j, step - 1].wait_recv()
             if step < count - 1:
@@ -89,43 +89,89 @@
                 steps[j, step] = copy
             share = remote(src, dst, core_send.at[j, step], core_recv.at[j, step], sibling, feat)
             share.start()
-            pending.append(share)
+            shares.append(share)
         if step == 0:
-            for swap in pending[: parts + 1]:
+            for swap in swaps:
                 swap.start()
-            own = pltpu.make_async_copy(feats, all_feats.at[me], own_sem)
+            own = pltpu.make_async_copy(feats, held.at[pl.ds(me * rows, rows)], own_sem.at[0])
             own.start()
-    own.wait()
-    for copy in steps.values():
+            own_tiles = pltpu.make_async_copy(tiles, tiles_a, own_sem.at[1])
+            own_tiles.start()
+    swaps[parts].wait_recv()
+    load_cols = pltpu.make_async_copy(all_cols, cols_b, own_sem.at[2])
+    load_cols.start()
+    for swap in swaps[:parts]:
+        swap.wait_recv()
+    keep_tiles = pltpu.make_async_copy(tiles_b, all_tiles, own_sem.at[3])
+    keep_tiles.start()
+    for copy in (load_cols, own, own_tiles):
+        copy.wait()
+    for share in shares:
+        share.wait_recv()
+
+    groups = agg_send.shape[0]
+    group = rows // groups
+    outs = []
+    for g in range(groups):
+
+        @pl.loop(0, group // 2)
+        def _(i, g=g):
+            for r in (g * group + 2 * i, g * group + 2 * i + 1):
+                acc = jnp.zeros(total.shape[1:], F32)
+                for names, block in ((cols_here, tiles_a), (cols_b, tiles_b)):
+                    for k in range(tiles.shape[1]):
+                        acc += jnp.dot(block[r, k], held[names[r, k]], preferred_element_type=F32)
+                total[r] = acc.astype(BF16)
+
+        piece = pl.ds(g * group, group)
+        copy = remote(
+            total.at[piece], agg_b.at[piece], agg_send.at[g], agg_recv.at[g], me, 1 - feat
+        )
+        copy.start()
+        keep = pltpu.make_async_copy(total.at[piece], agg.at[piece], keep_sem.at[g])
+        keep.start()
+        outs.append((copy, keep))
+    for copy, keep in outs:
+        keep.wait()
+        copy.wait_recv()
         copy.wait_send()
-    for copy in pending:
+    keep_tiles.wait()
+    for copy in (*steps.values(), *shares, *swaps):
         copy.wait_send()
-        copy.wait_recv()
-
-
-def gather_all(features, tile_vals, block_cols, n_node):
+
+
+def gather_spread(features, tile_vals, block_cols, n_node):
     any_space = pl.BlockSpec(memory_space=pl.ANY)
     count = n_node // 2
     dma = pltpu.SemaphoreType.DMA
+    rows = features.shape[0]
+    agg = jax.ShapeDtypeStruct(features.shape, BF16)
     return pl.pallas_call(
         functools.partial(gather_kernel, n_node),
         out_shape=(
-            jax.ShapeDtypeStruct((n_node, *features.shape), features.dtype),
+            agg,
+            agg,
             jax.ShapeDtypeStruct(tile_vals.shape, tile_vals.dtype),
             jax.ShapeDtypeStruct(block_cols.shape, block_cols.dtype),
         ),
-        in_specs=[any_space] * 3,
-        out_specs=[any_space] * 3,
+        in_specs=[any_space] * 3 + [pl.BlockSpec(memory_space=pltpu.SMEM)],
+        out_specs=[any_space] * 4,
         scratch_shapes=[
+            pltpu.VMEM((n_node * rows, *features.shape[1:]), BF16),
+            pltpu.VMEM(tile_vals.shape, BF16),
+            pltpu.VMEM(tile_vals.shape, BF16),
+            pltpu.SMEM(block_cols.shape, jnp.int32),
+            pltpu.VMEM(features.shape, BF16),
             dma((STREAMS, count - 1)), dma((STREAMS, count - 1)),
             dma((STREAMS, count)), dma((STREAMS, count)),
-            dma, dma((5,)), dma((5,)),
+            dma((4,)), dma((5,)), dma((5,)),
+            dma((4,)), dma((4,)), dma((4,)),
         ],
         compiler_params=pltpu.CompilerParams(
-            collective_id=0, has_side_effects=True, vmem_limit_bytes=4 << 20
-        ),
-        name="gather_ring",
-    )(features, tile_vals, block_cols)
+            collective_id=0, has_side_effects=True, vmem_limit_bytes=60 << 20
+        ),
+        name="gather_spread",
+    )(features, tile_vals, block_cols, block_cols)
 
 
 def scatter_kernel(
@@ -270,46 +316,6 @@
     )(part, weight_part)
 
 
-def spread_kernel(group, cols_a, cols_b, tiles_a, tiles_b, feats, out):
-    base = pl.program_id(0) * group
-    for r in range(group):
-        total = jnp.zeros(out.shape[1:], F32)
-        for cols, tiles in ((cols_a, tiles_a), (cols_b, tiles_b)):
-            for k in range(tiles.shape[1]):
-                total += jnp.dot(
-                    tiles[r, k], feats[cols[base + r, k]], preferred_element_type=F32
-                )
-        out[r] = total.astype(BF16)
-
-
-def spread(cols_a, cols_b, tiles_a, tiles_b, feats):
-    rows, slots, side, _ = tiles_a.shape
-    blocks, _, width = feats.shape
-    group = math.gcd(rows, 4)
-    tile_spec = pl.BlockSpec((group, slots, side, side), lambda i, *_: (i, 0, 0, 0))
-    return pl.pallas_call(
-        functools.partial(spread_kernel, group),
-        out_shape=jax.ShapeDtypeStruct((rows, side, width), BF16),
-        grid_spec=pltpu.PrefetchScalarGridSpec(
-            num_scalar_prefetch=2,
-            grid=(rows // group,),
-            in_specs=[
-                tile_spec,
-                tile_spec,
-                pl.BlockSpec((blocks, side, width), lambda i, *_: (0, 0, 0), pipeline_mode=pl.Buffered(1)),
-            ],
-            out_specs=pl.BlockSpec((group, side, width), lambda i, *_: (i, 0, 0)),
-        ),
-        compiler_params=pltpu.CompilerParams(vmem_limit_bytes=60 << 20),
-        cost_estimate=pl.CostEstimate(
-            flops=4 * rows * slots * side * side * width,
-            bytes_accessed=2 * (feats.size + 2 * tiles_a.size),
-            transcendentals=0,
-        ),
-        name="spread",
-    )(cols_a, cols_b, tiles_a, tiles_b, feats)
-
-
 def collect_kernel(group, cols_a, cols_b, tiles_a, tiles_b, grads, part):
     @pl.when(pl.program_id(0) == 0)
     def _():
@@ -371,11 +377,10 @@
     def dot(a, b):
         return jnp.dot(a, b, preferred_element_type=F32)
 
-    all_feats, tiles_b, cols_b = gather_all(features, tile_vals, block_cols, n_node)
-    agg = spread(
-        block_cols, cols_b, tile_vals, tiles_b, all_feats.reshape(blocks, side, width)
-    ).reshape(nodes, width)
-    agg_b = lax.ppermute(agg, "feat", swap)
+    agg, agg_b, tiles_b, cols_b = gather_spread(
+        features.reshape(rows, side, width), tile_vals, block_cols, n_node
+    )
+    agg, agg_b = agg.reshape(nodes, width), agg_b.reshape(nodes, width)
     other = 1 - feat
     pre_act = dot(agg, w_block(feat, feat)) + dot(agg_b, w_block(other, feat))
     gate = jax.nn.sigmoid(pre_act)

time: 416 us -> 384 us (0.923)
  waiting for transfers between devices: 63.7 us -> 30.5 us
  Pallas kernels: 318 us -> 336 us
  local copies, waits for them, and re-layouts: 18.4 us -> 4.22 us
    ppermute x1 -> x0, waiting for transfers between devices: 33 us -> none  [per_device_pair(): agg_b = lax.ppermute(agg, 'feat', swap)]
    pallas_call x2 -> x1, Pallas kernels: 162 us -> 180 us  [gather_spread(): pl.pallas_call(functools.partial(gather_kernel, n_node), out_shape=(agg,...]
    unnamed x23 -> x11, local copies, waits for them, and re-layouts: 18.4 us -> 4.22 us
  transfers between devices with their start and end apart: 2 -> 1, of which waited for: 2 -> 1; matrix products, arithmetic and copies ran while one was open for 1% -> 0% of each run, Pallas kernels for 0% -> 0%
where the time goes in v3:
time: 384 us
  Pallas kernels  336 us (88%)
  waiting for transfers between devices  30.5 us (8%)
  matrix products  10.2 us (3%)
  local copies, waits for them, and re-layouts  4.22 us (1%)
    pallas_call x1, Pallas kernels, gather_spread(): pl.pallas_call(functools.partial(gather_kernel, n_node), out_shape=(agg,...  180 us
    pallas_call x1, Pallas kernels, scatter_sum(): pl.pallas_call(functools.partial(scatter_kernel, n_node, scale), out_shap...  131 us
    ppermute x1, waiting for transfers between devices, per_device_pair(): grad_pre_b = lax.ppermute(grad_pre, 'feat', swap)  30.5 us
    pallas_call x1, Pallas kernels, collect(): pl.pallas_call(functools.partial(collect_kernel, group), out_shape=jax.Sh...  25.4 us
    dot_general x6, matrix products, dot(): return jnp.dot(a, b, preferred_element_type=F32)  10.2 us
  transfers between devices with their start and end apart: 1, of which 1 were waited for; matrix products, arithmetic and copies ran while one was open for 0% of the time, Pallas kernels for 0%

profile of v3, /device:TPU:0, one launch (start us, length us, event | category | flops | bytes accessed | tf_op | source)
XLA Modules:
  0.0 383.6 jit_solution(16476722728697276284)
XLA Ops:
  0.6 0.0 copy-start
  0.7 1.4 copy.8.cols.cols_here.cols_a
  2.1 180.0 %gather_spread.1 = (bf16[48,128,128]{2,1,0:T(8,128)(2,1)}, bf16[48,128,128]{2,1,0:T(8,128)(2,1)}, bf16[48,4,128,128]{3,2,1,0:T(8,128)(2,1)}, s32[48,4]{1,0:T(8,128)}) custom-call(bf16[48,128,128]{2,1,0:T(8,128)(2,1)} %bitcast.19, bf16[48,4,128,128]{3,2,1,0:T(8,128)(2,1)} %tiles_a.1, s32[48,4]{1,0:T(8,128)} %copy.8.cols.cols_here.cols_a, ...), custom_call_target="tpu_custom_call" | custom-call | tf_op jit(solution)/shard_map/gather_spread/pallas_call | solution.py:149
  182.1 0.0 copy-done
  182.1 0.0 copy-start.2
  182.1 0.0 copy-start.3
  182.1 2.1 fusion.5
  184.3 0.0 copy-done.2
  184.3 0.2 copy-done.3
  184.5 3.1 multiply_convert_fusion
  187.6 1.5 collective-permute-start
  189.1 0.0 copy-start.1
  189.1 0.6 fusion.8
  189.7 0.8 copy-done.1
  190.5 0.6 fusion.7
  191.2 0.6 fusion.3
  191.7 30.5 %collective-permute-done = bf16[6144,128]{1,0:T(8,128)(2,1)} collective-permute-done((bf16[6144,128]{1,0:T(8,128)(2,1)S(1)}, bf16[6144,128]{1,0:T(8,128)(2,1)}, u32[]{:S(2)}, u32[]{:S(2)}) %collective-permute-start) | collective-permute-done | bytes 1572896 | tf_op jit(solution)/shard_map/ppermute | solution.py:389
  222.2 3.2 fusion
  225.4 25.4 %collect.1 = bf16[768,128,128]{2,1,0:T(8,128)(2,1)} custom-call(s32[48,4]{1,0:T(8,128)} %copy.8.cols.cols_here.cols_a, s32[48,4]{1,0:T(8,128)} %get-tuple-element.11.cols_b, bf16[48,4,128,128]{3,2,1,0:T(8,128)(2,1)} %tiles_a.1, bf16[48,4,128,128]{3,2,1,0:T(8,128)(2,1)} %get-tuple-element.12.tiles_b, bf16[48,128,128]{2,1,0:T(8,128)(2,1)} %bitcast.16), custom_call_target="tpu_custom_call" | custom-call | flops 1610612736 | bytes 37748736 | tf_op jit(solution)/shard_map/collect/pallas_call | solution.py:342
  250.8 130.9 %scatter_ring.1 = (bf16[6144,128]{1,0:T(8,128)(2,1)S(1)}, f32[256,128]{1,0:T(8,128)S(1)}) custom-call(bf16[16,6144,128]{2,1,0:T(8,128)(2,1)} %bitcast.13, f32[256,128]{1,0:T(8,128)S(1)} %maximum_select_fusion.weight_part), custom_call_target="tpu_custom_call" | custom-call | tf_op jit(solution)/shard_map/scatter_ring/pallas_call | solution.py:293
  381.8 0.7 copy.13
  382.4 1.1 copy.14
  (1 shorter events, 0.0 us)
Async XLA Ops:
  0.6 181.5 %copy-start = (bf16[256,256]{1,0:T(8,128)(2,1)S(1)}, bf16[256,256]{1,0:T(8,128)(2,1)}, u32[]{:S(2)}) copy-start(bf16[256,256]{1,0:T(8,128)(2,1)} %param.8) | copy-start | bytes 393220
  182.1 2.1 copy-start.2
  182.1 2.3 copy-start.3
  187.6 34.6 %collective-permute-start = (bf16[6144,128]{1,0:T(8,128)(2,1)S(1)}, bf16[6144,128]{1,0:T(8,128)(2,1)}, u32[]{:S(2)}, u32[]{:S(2)}) collective-permute-start(bf16[6144,128]{1,0:T(8,128)(2,1)S(1)} %get-tuple-element.15), channel_id=1, source_target_pairs={{0,1},{1,0},{2,3},{3,2},{4,5},{5,4},{6,7},{7,6},{8,9},{9,8},{10,11... | collective-permute-start | bytes 4718600 | tf_op jit(solution)/shard_map/ppermute | solution.py:389
  189.1 1.4 copy-start.1

commit v4 on v3

--- a/solution.py
+++ b/solution.py
@@ -47,10 +47,10 @@
 
 
 def gather_kernel(
-    n_node, feats, tiles, cols, cols_here, agg, agg_b, all_tiles, all_cols,
+    n_node, feats, tiles, cols, cot, cols_here, agg, agg_b, cot_b, all_tiles, all_cols,
     held, tiles_a, tiles_b, cols_b, total,
     ring_send, ring_recv, core_send, core_recv, own_sem, swap_send, swap_recv,
-    agg_send, agg_recv, keep_sem,
+    agg_send, agg_recv, keep_sem, cot_send, cot_recv,
 ):
     me, core, pos, depth = ring_here(n_node)
     feat = lax.axis_index("feat")
@@ -71,6 +71,9 @@
         )
     swaps.append(remote(cols, all_cols, swap_send.at[parts], swap_recv.at[parts], me, 1 - feat))
 
+    part_rows = rows // 2
+    mine = pl.ds(feat * part_rows, part_rows)
+    theirs = pl.ds((1 - feat) * part_rows, part_rows)
     targets = (right, left)
     steps, shares = {}, []
     for step in range(count):
@@ -93,6 +96,8 @@
         if step == 0:
             for swap in swaps:
                 swap.start()
+            cot_copy = remote(cot.at[theirs], cot_b, cot_send, cot_recv, me, 1 - feat)
+            cot_copy.start()
             own = pltpu.make_async_copy(feats, held.at[pl.ds(me * rows, rows)], own_sem.at[0])
             own.start()
             own_tiles = pltpu.make_async_copy(tiles, tiles_a, own_sem.at[1])
@@ -109,30 +114,33 @@
     for share in shares:
         share.wait_recv()
 
-    groups = agg_send.shape[0]
-    group = rows // groups
-    outs = []
-    for g in range(groups):
-
-        @pl.loop(0, group // 2)
-        def _(i, g=g):
-            for r in (g * group + 2 * i, g * group + 2 * i + 1):
+    def multiply(first, amount):
+        @pl.loop(0, amount // 2)
+        def _(i):
+            for r in (first + 2 * i, first + 2 * i + 1):
                 acc = jnp.zeros(total.shape[1:], F32)
                 for names, block in ((cols_here, tiles_a), (cols_b, tiles_b)):
                     for k in range(tiles.shape[1]):
                         acc += jnp.dot(block[r, k], held[names[r, k]], preferred_element_type=F32)
                 total[r] = acc.astype(BF16)
 
-        piece = pl.ds(g * group, group)
+    groups = agg_send.shape[0]
+    group = part_rows // groups
+    outs = []
+    for g in range(groups):
+        first = (1 - feat) * part_rows + g * group
+        multiply(first, group)
         copy = remote(
-            total.at[piece], agg_b.at[piece], agg_send.at[g], agg_recv.at[g], me, 1 - feat
+            total.at[pl.ds(first, group)], agg_b.at[pl.ds(g * group, group)],
+            agg_send.at[g], agg_recv.at[g], me, 1 - feat,
         )
         copy.start()
-        keep = pltpu.make_async_copy(total.at[piece], agg.at[piece], keep_sem.at[g])
-        keep.start()
-        outs.append((copy, keep))
-    for copy, keep in outs:
-        keep.wait()
+        outs.append(copy)
+    multiply(feat * part_rows, part_rows)
+    keep = pltpu.make_async_copy(total.at[mine], agg, keep_sem)
+    keep.start()
+    keep.wait()
+    for copy in (cot_copy, *outs):
         copy.wait_recv()
         copy.wait_send()
     keep_tiles.wait()
@@ -140,22 +148,23 @@
         copy.wait_send()
 
 
-def gather_spread(features, tile_vals, block_cols, n_node):
+def gather_spread(features, tile_vals, block_cols, cotangent, n_node):
     any_space = pl.BlockSpec(memory_space=pl.ANY)
     count = n_node // 2
     dma = pltpu.SemaphoreType.DMA
     rows = features.shape[0]
-    agg = jax.ShapeDtypeStruct(features.shape, BF16)
+    agg = jax.ShapeDtypeStruct((rows // 2, *features.shape[1:]), BF16)
     return pl.pallas_call(
         functools.partial(gather_kernel, n_node),
         out_shape=(
             agg,
             agg,
+            agg,
             jax.ShapeDtypeStruct(tile_vals.shape, tile_vals.dtype),
             jax.ShapeDtypeStruct(block_cols.shape, block_cols.dtype),
         ),
-        in_specs=[any_space] * 3 + [pl.BlockSpec(memory_space=pltpu.SMEM)],
-        out_specs=[any_space] * 4,
+        in_specs=[any_space] * 4 + [pl.BlockSpec(memory_space=pltpu.SMEM)],
+        out_specs=[any_space] * 5,
         scratch_shapes=[
             pltpu.VMEM((n_node * rows, *features.shape[1:]), BF16),
             pltpu.VMEM(tile_vals.shape, BF16),
@@ -165,13 +174,13 @@
             dma((STREAMS, count - 1)), dma((STREAMS, count - 1)),
             dma((STREAMS, count)), dma((STREAMS, count)),
             dma((4,)), dma((5,)), dma((5,)),
-            dma((4,)), dma((4,)), dma((4,)),
+            dma((4,)), dma((4,)), dma, dma, dma,
         ],
         compiler_params=pltpu.CompilerParams(
             collective_id=0, has_side_effects=True, vmem_limit_bytes=60 << 20
         ),
         name="gather_spread",
-    )(features, tile_vals, block_cols, block_cols)
+    )(features, tile_vals, block_cols, cotangent, block_cols)
 
 
 def scatter_kernel(
@@ -371,29 +380,40 @@
     feat = lax.axis_index("feat")
     swap = [(0, 1), (1, 0)]
 
-    def w_block(i, j):
-        return lax.dynamic_slice(weight, (i * width, j * width), (width, width))
-
     def dot(a, b):
         return jnp.dot(a, b, preferred_element_type=F32)
 
-    agg, agg_b, tiles_b, cols_b = gather_spread(
-        features.reshape(rows, side, width), tile_vals, block_cols, n_node
+    def in_order(here, there, axis):
+        return jnp.where(
+            feat == 0,
+            jnp.concatenate([here, there], axis),
+            jnp.concatenate([there, here], axis),
+        )
+
+    def columns(array, index):
+        return lax.dynamic_slice_in_dim(array, index * width, width, 1)
+
+    other = 1 - feat
+    half = nodes // 2
+    agg, agg_b, cot_b, tiles_b, cols_b = gather_spread(
+        features.reshape(rows, side, width), tile_vals, block_cols,
+        cotangent.reshape(rows, side, width), n_node,
     )
-    agg, agg_b = agg.reshape(nodes, width), agg_b.reshape(nodes, width)
-    other = 1 - feat
-    pre_act = dot(agg, w_block(feat, feat)) + dot(agg_b, w_block(other, feat))
+    agg, agg_b, cot_b = (x.reshape(half, width) for x in (agg, agg_b, cot_b))
+    cot = lax.dynamic_slice_in_dim(cotangent, feat * half, half, 0)
+    agg, cot = in_order(agg, agg_b, 1), in_order(cot, cot_b, 1)
+    pre_act = dot(agg, weight)
     gate = jax.nn.sigmoid(pre_act)
-    activated = (pre_act * gate).astype(BF16)
-    grad_pre = (cotangent.astype(F32) * gate * (1.0 + pre_act * (1.0 - gate))).astype(BF16)
-    grad_pre_b = lax.ppermute(grad_pre, "feat", swap)
-    grad_agg = (
-        dot(grad_pre, w_block(feat, feat).T) + dot(grad_pre_b, w_block(feat, other).T)
-    ).astype(BF16)
-    mine, theirs = dot(agg.T, grad_pre), dot(agg_b.T, grad_pre)
-    local = jnp.where(
-        feat == 0, jnp.concatenate([mine, theirs]), jnp.concatenate([theirs, mine])
-    )
+    act = (pre_act * gate).astype(BF16)
+    grad_pre = (cot.astype(F32) * gate * (1.0 + pre_act * (1.0 - gate))).astype(BF16)
+    grad_agg = dot(grad_pre, weight.T).astype(BF16)
+    grad_agg_b = lax.ppermute(columns(grad_agg, other), "feat", swap)
+    local = dot(agg.T, grad_pre)
+    local = columns(local, feat) + lax.ppermute(columns(local, other), "feat", swap)
+    act_there, grad_agg_b = lax.optimization_barrier((columns(act, other), grad_agg_b))
+    act_b = lax.ppermute(act_there, "feat", swap)
+    activated = in_order(columns(act, feat), act_b, 0)
+    grad_agg = in_order(columns(grad_agg, feat), grad_agg_b, 0)
     part = collect(
         block_cols, cols_b, tile_vals, tiles_b, grad_agg.reshape(rows, side, width), blocks
     )

time: 384 us -> 370 us (0.964)
  waiting for transfers between devices: 30.5 us -> 18.3 us
  matrix products: 10.2 us -> 5.41 us
    ppermute x1 -> x3, waiting for transfers between devices: 30.5 us -> 18.3 us  [the longest x1 18.3 us: per_device_pair(): lax.ppermute(columns(local, other), 'feat', swap)]
    dot_general x6 -> x3, matrix products: 10.2 us -> 5.41 us  [dot(): return jnp.dot(a, b, preferred_element_type=F32)]
  transfers between devices with their start and end apart: 1 -> 3, of which waited for: 1 -> 1; matrix products, arithmetic and copies ran while one was open for 0% -> 1% of each run, Pallas kernels for 0% -> 42%
where the time goes in v4:
time: 370 us; the launch traced here: 369 us
  Pallas kernels  333 us (90%)
  waiting for transfers between devices  18.3 us (5%)
  local copies, waits for them, and re-layouts  6.9 us (2%)
  matrix products  5.41 us (1%)
    pallas_call x1, Pallas kernels, gather_spread(): pl.pallas_call(functools.partial(gather_kernel, n_node), out_shape=(agg,...  177 us
    pallas_call x1, Pallas kernels, scatter_sum(): pl.pallas_call(functools.partial(scatter_kernel, n_node, scale), out_shap...  131 us
    pallas_call x1, Pallas kernels, collect(): pl.pallas_call(functools.partial(collect_kernel, group), out_shape=jax.Sh...  25.4 us
    ppermute x1, waiting for transfers between devices, per_device_pair(): lax.ppermute(columns(local, other), 'feat', swap)  18.3 us
  transfers between devices with their start and end apart: 3, of which 1 were waited for; matrix products, arithmetic and copies ran while one was open for 1% of the time, Pallas kernels for 42%

profile of v4, /device:TPU:0, one launch (start us, length us, event | category | flops | bytes accessed | tf_op | source)
XLA Modules:
  0.0 369.4 jit_solution(322339623366731880)
XLA Ops:
  0.6 0.0 copy-start
  0.7 1.4 copy.8.cols.cols_here.cols_a
  2.1 1.2 constant_dynamic-slice_fusion.3
  3.3 176.9 %gather_spread.1 = (bf16[24,128,128]{2,1,0:T(8,128)(2,1)}, bf16[24,128,128]{2,1,0:T(8,128)(2,1)}, bf16[24,128,128]{2,1,0:T(8,128)(2,1)}, bf16[48,4,128,128]{3,2,1,0:T(8,128)(2,1)}, s32[48,4]{1,0:T(8,128)}) custom-call(bf16[48,128,128]{2,1,0:T(8,128)(2,1)} %bitcast.14, bf16[48,4,128,128]{3,2,1,0:T(8,128)(2,1)} %tiles_a.1, s32[48,4]{1,0:T(8,128)} %copy.8.cols.cols_here.cols_a, ...), custom_call_target="tpu_custom_call" | custom-call | tf_op jit(solution)/shard_map/gather_spread/pallas_call | solution.py:157
  180.1 0.0 copy-done
  180.1 4.2 %multiply_convert_fusion = (bf16[3072,256]{1,0:T(8,128)(2,1)S(1)}, bf16[3072,256]{1,0:T(8,128)(2,1)S(1)}) fusion(bf16[3072,128]{1,0:T(8,128)(2,1)} %bitcast.19, bf16[3072,128]{1,0:T(8,128)(2,1)S(1)} %constant_dynamic-slice_fusion.3, pred[]{:T(512)S(6)} %eq.2, bf16[256,256]{1,0:T(8,128)(2,1)S(1)} %copy-done, bf16[3072,128]{1,0:T(8,128)(2,1)} %bitcast.17, ...), kind=kOutput, calls=%fused_computation.1 | convolution fusion | flops 426246144 | bytes 6422529 | tf_op jit(solution)/shard_map/dot_general | solution.py:384
  184.4 0.0 copy-start.1
  184.4 1.1 copy-done.1
  185.5 0.6 convolution_convert_fusion
  186.1 0.0 copy-start.2
  186.1 0.0 copy-start.3
  186.1 0.0 copy-start.4
  186.1 0.1 constant_dynamic-slice_fusion.1
  186.3 0.6 collective-permute-start
  186.8 0.7 copy-done.2
  187.5 0.2 copy-done.3
  187.7 0.2 copy-done.4
  187.9 0.6 fusion
  188.6 0.6 collective-permute-start.2
  189.2 0.1 constant_dynamic-slice_fusion.5
  189.3 18.3 %collective-permute-done.2 = f32[256,128]{1,0:T(8,128)S(1)} collective-permute-done((f32[256,128]{1,0:T(8,128)S(1)}, f32[256,128]{1,0:T(8,128)S(1)}, u32[]{:S(2)}, u32[]{:S(2)}) %collective-permute-start.2) | collective-permute-done | bytes 131104 | tf_op jit(solution)/shard_map/ppermute | solution.py:412
  207.6 0.0 collective-permute-done
  207.6 0.6 collective-permute-start.1
  208.2 1.5 maximum_select_fusion.3
  209.7 25.4 %collect.1 = bf16[768,128,128]{2,1,0:T(8,128)(2,1)} custom-call(s32[48,4]{1,0:T(8,128)} %copy.8.cols.cols_here.cols_a, s32[48,4]{1,0:T(8,128)} %get-tuple-element.16.cols_b, bf16[48,4,128,128]{3,2,1,0:T(8,128)(2,1)} %tiles_a.1, bf16[48,4,128,128]{3,2,1,0:T(8,128)(2,1)} %get-tuple-element.17.tiles_b, bf16[48,128,128]{2,1,0:T(8,128)(2,1)} %bitcast.12), custom_call_target="tpu_custom_call" | custom-call | flops 1610612736 | bytes 37748736 | tf_op jit(solution)/shard_map/collect/pallas_call | solution.py:351
  235.1 130.9 %scatter_ring.1 = (bf16[6144,128]{1,0:T(8,128)(2,1)S(1)}, f32[256,128]{1,0:T(8,128)S(1)}) custom-call(bf16[16,6144,128]{2,1,0:T(8,128)(2,1)} %bitcast.11, f32[256,128]{1,0:T(8,128)S(1)} %dynamic-slice_add_fusion.weight_part), custom_call_target="tpu_custom_call" | custom-call | tf_op jit(solution)/shard_map/scatter_ring/pallas_call | solution.py:302
  366.1 0.0 collective-permute-done.1
  366.1 1.6 maximum_select_fusion.2
  367.6 0.7 copy.13
  368.3 1.1 copy.14
  (2 shorter events, 0.0 us)
Async XLA Ops:
  0.6 179.5 %copy-start = (bf16[256,256]{1,0:T(8,128)(2,1)S(1)}, bf16[256,256]{1,0:T(8,128)(2,1)}, u32[]{:S(2)}) copy-start(bf16[256,256]{1,0:T(8,128)(2,1)} %param.8) | copy-start | bytes 393220
  184.4 1.1 copy-start.1
  186.1 1.4 copy-start.2
  186.1 1.6 copy-start.3
  186.1 1.8 copy-start.4
  186.3 21.3 %collective-permute-start = (bf16[3072,128]{1,0:T(8,128)(2,1)S(1)}, bf16[3072,128]{1,0:T(8,128)(2,1)S(1)}, u32[]{:S(2)}, u32[]{:S(2)}) collective-permute-start(bf16[3072,128]{1,0:T(8,128)(2,1)S(1)} %get-tuple-element.24), channel_id=1, source_target_pairs={{0,1},{1,0},{2,3},{3,2},{4,5},{5,4},{6,7},{7,6},{8,9},{9,8},{10,11... | collective-permute-start | bytes 2359304 | tf_op jit(solution)/shard_map/ppermute | solution.py:410
  188.6 19.0 %collective-permute-start.2 = (f32[256,128]{1,0:T(8,128)S(1)}, f32[256,128]{1,0:T(8,128)S(1)}, u32[]{:S(2)}, u32[]{:S(2)}) collective-permute-start(f32[256,128]{1,0:T(8,128)S(1)} %constant_dynamic-slice_fusion), channel_id=1, source_target_pairs={{0,1},{1,0},{2,3},{3,2},{4,5},{5,4},{6,7},{7,6},{8,9},{9,8},{10,11... | collective-permute-start | bytes 393224 | tf_op jit(solution)/shard_map/ppermute | solution.py:412
  207.6 158.5 %collective-permute-start.1 = (bf16[3072,128]{1,0:T(8,128)(2,1)S(1)}, bf16[3072,128]{1,0:T(8,128)(2,1)S(1)}, u32[]{:S(2)}, u32[]{:S(2)}) collective-permute-start(bf16[3072,128]{1,0:T(8,128)(2,1)S(1)} %get-tuple-element.15), channel_id=1, source_target_pairs={{0,1},{1,0},{2,3},{3,2},{4,5},{5,4},{6,7},{7,6},{8,9},{9,8},{10,11... | collective-permute-start | bytes 2359304 | tf_op jit(solution)/shard_map/ppermute | solution.py:414

commit v5 on v4

--- a/solution.py
+++ b/solution.py
@@ -65,7 +65,8 @@
     parts = swap_send.shape[0] - 1
     swaps = []
     for i in range(parts):
-        piece = pl.ds(i * (rows // parts), rows // parts)
+        start = (feat if i < parts // 2 else 1 - feat) * (rows // 2)
+        piece = pl.ds(start + i % (parts // 2) * (rows // parts), rows // parts)
         swaps.append(
             remote(tiles.at[piece], tiles_b.at[piece], swap_send.at[i], swap_recv.at[i], me, 1 - feat)
         )
@@ -94,21 +95,24 @@
             share.start()
             shares.append(share)
         if step == 0:
-            for swap in swaps:
+            swaps[parts].start()
+            for swap in swaps[: parts // 2]:
                 swap.start()
             cot_copy = remote(cot.at[theirs], cot_b, cot_send, cot_recv, me, 1 - feat)
-            cot_copy.start()
             own = pltpu.make_async_copy(feats, held.at[pl.ds(me * rows, rows)], own_sem.at[0])
             own.start()
             own_tiles = pltpu.make_async_copy(tiles, tiles_a, own_sem.at[1])
             own_tiles.start()
+        if step == 3:
+            for swap in swaps[parts // 2 : parts]:
+                swap.start()
+        if step == count - 2:
+            cot_copy.start()
     swaps[parts].wait_recv()
     load_cols = pltpu.make_async_copy(all_cols, cols_b, own_sem.at[2])
     load_cols.start()
-    for swap in swaps[:parts]:
+    for swap in swaps[: parts // 2]:
         swap.wait_recv()
-    keep_tiles = pltpu.make_async_copy(tiles_b, all_tiles, own_sem.at[3])
-    keep_tiles.start()
     for copy in (load_cols, own, own_tiles):
         copy.wait()
     for share in shares:
@@ -136,6 +140,10 @@
         )
         copy.start()
         outs.append(copy)
+    for swap in swaps[parts // 2 : parts]:
+        swap.wait_recv()
+    keep_tiles = pltpu.make_async_copy(tiles_b, all_tiles, own_sem.at[3])
+    keep_tiles.start()
     multiply(feat * part_rows, part_rows)
     keep = pltpu.make_async_copy(total.at[mine], agg, keep_sem)
     keep.start()

time: 370 us -> 370 us (level)
  no operation moved by 1% of the time
where the time goes in v5:
time: 370 us; the launch traced here: 369 us
  Pallas kernels  333 us (90%)
  waiting for transfers between devices  18.3 us (5%)
  local copies, waits for them, and re-layouts  6.9 us (2%)
  matrix products  5.41 us (1%)
    pallas_call x1, Pallas kernels, gather_spread(): pl.pallas_call(functools.partial(gather_kernel, n_node), out_shape=(agg,...  177 us
    pallas_call x1, Pallas kernels, scatter_sum(): pl.pallas_call(functools.partial(scatter_kernel, n_node, scale), out_shap...  131 us
    pallas_call x1, Pallas kernels, collect(): pl.pallas_call(functools.partial(collect_kernel, group), out_shape=jax.Sh...  25.4 us
    ppermute x1, waiting for transfers between devices, per_device_pair(): lax.ppermute(columns(local, other), 'feat', swap)  18.3 us
  transfers between devices with their start and end apart: 3, of which 1 were waited for; matrix products, arithmetic and copies ran while one was open for 1% of the time, Pallas kernels for 42%

profile of v5, /device:TPU:0, one launch (start us, length us, event | category | flops | bytes accessed | tf_op | source)
XLA Modules:
  0.0 369.4 jit_solution(14484542438400126192)
XLA Ops:
  0.6 0.0 copy-start
  0.7 1.4 copy.8.cols.cols_here.cols_a
  2.1 1.2 constant_dynamic-slice_fusion.3
  3.3 176.9 %gather_spread.1 = (bf16[24,128,128]{2,1,0:T(8,128)(2,1)}, bf16[24,128,128]{2,1,0:T(8,128)(2,1)}, bf16[24,128,128]{2,1,0:T(8,128)(2,1)}, bf16[48,4,128,128]{3,2,1,0:T(8,128)(2,1)}, s32[48,4]{1,0:T(8,128)}) custom-call(bf16[48,128,128]{2,1,0:T(8,128)(2,1)} %bitcast.14, bf16[48,4,128,128]{3,2,1,0:T(8,128)(2,1)} %tiles_a.1, s32[48,4]{1,0:T(8,128)} %copy.8.cols.cols_here.cols_a, ...), custom_call_target="tpu_custom_call" | custom-call | tf_op jit(solution)/shard_map/gather_spread/pallas_call | solution.py:165
  180.1 0.0 copy-done
  180.1 4.2 %multiply_convert_fusion = (bf16[3072,256]{1,0:T(8,128)(2,1)S(1)}, bf16[3072,256]{1,0:T(8,128)(2,1)S(1)}) fusion(bf16[3072,128]{1,0:T(8,128)(2,1)} %bitcast.19, bf16[3072,128]{1,0:T(8,128)(2,1)S(1)} %constant_dynamic-slice_fusion.3, pred[]{:T(512)S(6)} %eq.2, bf16[256,256]{1,0:T(8,128)(2,1)S(1)} %copy-done, bf16[3072,128]{1,0:T(8,128)(2,1)} %bitcast.17, ...), kind=kOutput, calls=%fused_computation.1 | convolution fusion | flops 426246144 | bytes 6422529 | tf_op jit(solution)/shard_map/dot_general | solution.py:392
  184.4 0.0 copy-start.1
  184.4 1.1 copy-done.1
  185.5 0.6 convolution_convert_fusion
  186.1 0.0 copy-start.2
  186.1 0.0 copy-start.3
  186.1 0.0 copy-start.4
  186.1 0.1 constant_dynamic-slice_fusion.1
  186.3 0.6 collective-permute-start
  186.8 0.7 copy-done.2
  187.5 0.2 copy-done.3
  187.7 0.2 copy-done.4
  187.9 0.6 fusion
  188.6 0.6 collective-permute-start.2
  189.2 0.1 constant_dynamic-slice_fusion.5
  189.3 18.3 %collective-permute-done.2 = f32[256,128]{1,0:T(8,128)S(1)} collective-permute-done((f32[256,128]{1,0:T(8,128)S(1)}, f32[256,128]{1,0:T(8,128)S(1)}, u32[]{:S(2)}, u32[]{:S(2)}) %collective-permute-start.2) | collective-permute-done | bytes 131104 | tf_op jit(solution)/shard_map/ppermute | solution.py:420
  207.6 0.0 collective-permute-done
  207.6 0.6 collective-permute-start.1
  208.2 1.5 maximum_select_fusion.3
  209.7 25.4 %collect.1 = bf16[768,128,128]{2,1,0:T(8,128)(2,1)} custom-call(s32[48,4]{1,0:T(8,128)} %copy.8.cols.cols_here.cols_a, s32[48,4]{1,0:T(8,128)} %get-tuple-element.16.cols_b, bf16[48,4,128,128]{3,2,1,0:T(8,128)(2,1)} %tiles_a.1, bf16[48,4,128,128]{3,2,1,0:T(8,128)(2,1)} %get-tuple-element.17.tiles_b, bf16[48,128,128]{2,1,0:T(8,128)(2,1)} %bitcast.12), custom_call_target="tpu_custom_call" | custom-call | flops 1610612736 | bytes 37748736 | tf_op jit(solution)/shard_map/collect/pallas_call | solution.py:359
  235.1 130.9 %scatter_ring.1 = (bf16[6144,128]{1,0:T(8,128)(2,1)S(1)}, f32[256,128]{1,0:T(8,128)S(1)}) custom-call(bf16[16,6144,128]{2,1,0:T(8,128)(2,1)} %bitcast.11, f32[256,128]{1,0:T(8,128)S(1)} %dynamic-slice_add_fusion.weight_part), custom_call_target="tpu_custom_call" | custom-call | tf_op jit(solution)/shard_map/scatter_ring/pallas_call | solution.py:310
  366.1 0.0 collective-permute-done.1
  366.1 1.6 maximum_select_fusion.2
  367.6 0.7 copy.13
  368.3 1.1 copy.14
  (2 shorter events, 0.0 us)
Async XLA Ops:
  0.6 179.5 %copy-start = (bf16[256,256]{1,0:T(8,128)(2,1)S(1)}, bf16[256,256]{1,0:T(8,128)(2,1)}, u32[]{:S(2)}) copy-start(bf16[256,256]{1,0:T(8,128)(2,1)} %param.8) | copy-start | bytes 393220
  184.4 1.1 copy-start.1
  186.1 1.4 copy-start.2
  186.1 1.6 copy-start.3
  186.1 1.8 copy-start.4
  186.3 21.3 %collective-permute-start = (bf16[3072,128]{1,0:T(8,128)(2,1)S(1)}, bf16[3072,128]{1,0:T(8,128)(2,1)S(1)}, u32[]{:S(2)}, u32[]{:S(2)}) collective-permute-start(bf16[3072,128]{1,0:T(8,128)(2,1)S(1)} %get-tuple-element.24), channel_id=1, source_target_pairs={{0,1},{1,0},{2,3},{3,2},{4,5},{5,4},{6,7},{7,6},{8,9},{9,8},{10,11... | collective-permute-start | bytes 2359304 | tf_op jit(solution)/shard_map/ppermute | solution.py:418
  188.6 19.0 %collective-permute-start.2 = (f32[256,128]{1,0:T(8,128)S(1)}, f32[256,128]{1,0:T(8,128)S(1)}, u32[]{:S(2)}, u32[]{:S(2)}) collective-permute-start(f32[256,128]{1,0:T(8,128)S(1)} %constant_dynamic-slice_fusion), channel_id=1, source_target_pairs={{0,1},{1,0},{2,3},{3,2},{4,5},{5,4},{6,7},{7,6},{8,9},{9,8},{10,11... | collective-permute-start | bytes 393224 | tf_op jit(solution)/shard_map/ppermute | solution.py:420
  207.6 158.5 %collective-permute-start.1 = (bf16[3072,128]{1,0:T(8,128)(2,1)S(1)}, bf16[3072,128]{1,0:T(8,128)(2,1)S(1)}, u32[]{:S(2)}, u32[]{:S(2)}) collective-permute-start(bf16[3072,128]{1,0:T(8,128)(2,1)S(1)} %get-tuple-element.15), channel_id=1, source_target_pairs={{0,1},{1,0},{2,3},{3,2},{4,5},{5,4},{6,7},{7,6},{8,9},{9,8},{10,11... | collective-permute-start | bytes 2359304 | tf_op jit(solution)/shard_map/ppermute | solution.py:422
